TPU v7x, 32 devices: a whole 2x2x4 slice. The times are simulated.
32 devices in a mesh: blk: 8 (over z, x), uly: 4 (over y, core).
Axes of the slice: x: 2, y: 2, z: 4, core: 2. Of those that a mesh axis runs over, the one named last changes fastest.
Arguments:
- tokens: bfloat16 [768, 2560], P(('blk', 'uly')), may hold values from -6 to 6
- in_bits: int32 [768, 2560], P(('blk', 'uly')), may hold values from 0 to 1
- qkv_weights: bfloat16 [2, 3, 2560, 2560], P(None, None, 'blk', 'uly'), may hold values from -0.125 to 0.125
- qkv_bits: int32 [768, 3, 2560], P('blk', None, 'uly'), may hold values from 0 to 1
- gain_query: float32 [2560], P('uly'), may hold values from 0.7 to 1.8
- gain_key: float32 [2560], P('uly'), may hold values from 0.7 to 1.8
- out_weights: bfloat16 [2, 2560, 2560], P(None, 'uly', 'blk'), may hold values from -0.5 to 0.5
- mix_bits: int32 [768, 2560], P('blk', 'uly'), may hold values from 0 to 1
- out_bits: int32 [768, 2560], P('blk'), may hold values from 0 to 1
Outputs:
- layer_output: bfloat16 [768, 2560], P(('blk', 'uly'))
Inputs may be any that keep to these rules, and one draw needn't show every extreme that they name: `in_bits`: a bit of 1 stands for the sign +1, a bit of 0 for -1. `qkv_bits`: a bit of 1 stands for the sign +1, a bit of 0 for -1. `mix_bits`: a bit of 1 stands for the sign +1, a bit of 0 for -1. `out_bits`: a bit of 1 stands for the sign +1, a bit of 0 for -1.
All inputs are finite; a program needn't handle non-finite values.
Results may differ from a plain program's by a relative error of at most 0.018.
Values may be sent and summed in bfloat16 or wider, within the bound.
No kernel may reach another device: no remote copies, remote signals or barrier semaphores. Data moves between devices by JAX's collectives and lax.ppermute only.
A program may use at most 128 MiB of HBM per device.

v0:
```python
import functools
import math

import jax
import jax.numpy as jnp
from jax import lax
from jax.experimental import pallas as pl
from jax.experimental.pallas import tpu as pltpu
from jax.sharding import PartitionSpec as P

HEAD = 128


epsilon = 1e-06


def signed(bit_values):
    return (2 * bit_values - 1).astype(jnp.float32)


def normalize(values, gain_vector):
    row_count = values.shape[0]
    by_head = values.astype(jnp.float32).reshape(row_count, -1, HEAD)
    inverse_rms = lax.rsqrt(jnp.mean(by_head * by_head, axis=-1, keepdims=True) + epsilon)
    return (by_head * inverse_rms * gain_vector.reshape(-1, HEAD)).astype(jnp.bfloat16)


def gather_plan(
    tokens, in_bits, qkv_weights, qkv_bits, gain_query, gain_key, out_weights, mix_bits, out_bits
):
    flipped = (tokens.astype(jnp.float32) * signed(in_bits)).astype(jnp.bfloat16)
    group_rows = lax.all_gather(jnp.stack([tokens, flipped]), "uly", axis=1, tiled=True)
    row_total = group_rows.shape[1]
    projections = jnp.einsum(
        "mrd,mkdc->rmkc",
        group_rows,
        lax.all_gather(qkv_weights, "blk", axis=2, tiled=True),
        preferred_element_type=jnp.float32,
    )
    projected = (projections[:, 0] + signed(qkv_bits) * projections[:, 1]).astype(jnp.bfloat16)
    queries = normalize(projected[:, 0], gain_query)
    head_count = queries.shape[1]
    keys_normed = normalize(projected[:, 1], gain_key).reshape(row_total, -1)
    values_block = projected[:, 2]
    score_scale = 1.0 / math.sqrt(HEAD)

    def attend(running, shard_piece):
        numerator, denominator = running
        key_rows = shard_piece[0].reshape(shard_piece[0].shape[0], head_count, HEAD)
        value_rows = shard_piece[1].reshape(shard_piece[1].shape[0], head_count, HEAD)
        scores = (
            jnp.einsum("rhd,nhd->hrn", queries, key_rows, preferred_element_type=jnp.float32)
            * score_scale
        )
        weights = jnp.exp(scores).astype(jnp.bfloat16)
        numerator = numerator + jnp.einsum(
            "hrn,nhd->rhd", weights, value_rows, preferred_element_type=jnp.float32
        )
        denominator = denominator + jnp.sum(weights.astype(jnp.float32), axis=2).T
        return (numerator, denominator)

    start_state = (
        jnp.zeros((row_total, head_count, HEAD), jnp.float32),
        jnp.zeros((row_total, head_count), jnp.float32),
    )
    all_keys, all_values = (
        lax.all_gather(keys_normed, "blk", axis=0, tiled=True),
        lax.all_gather(values_block, "blk", axis=0, tiled=True),
    )
    group_count = lax.axis_size("blk")
    per_block = 1
    while per_block * row_total < 512 and group_count % (per_block * 2) == 0:
        per_block = per_block * 2
    block_rows = per_block * row_total
    block_count = group_count // per_block
    key_blocks = all_keys.reshape(block_count, block_rows, all_keys.shape[1])
    value_blocks = all_values.reshape(block_count, block_rows, all_values.shape[1])

    def scan_step(running, block_pair):
        return (attend(running, block_pair), None)

    (numerator, denominator), unused = lax.scan(scan_step, start_state, (key_blocks, value_blocks))
    attended = (numerator / denominator[:, :, None]).astype(jnp.bfloat16).reshape(row_total, -1)
    attended_flipped = (attended.astype(jnp.float32) * signed(mix_bits)).astype(jnp.bfloat16)
    attended_pair = jnp.stack([attended, attended_flipped])
    out_signs = signed(out_bits)
    partial_out = jnp.einsum(
        "mrc,mcn->rmn",
        attended_pair,
        lax.all_gather(out_weights, "blk", axis=2, tiled=True),
        preferred_element_type=jnp.float32,
    )
    summed = lax.psum_scatter(
        partial_out.astype(jnp.bfloat16), "uly", scatter_dimension=0, tiled=True
    ).astype(jnp.float32)
    own_rows = summed.shape[0]
    own_signs = lax.dynamic_slice_in_dim(out_signs, lax.axis_index("uly") * own_rows, own_rows, 0)
    result_rows = summed[:, 0] + own_signs * summed[:, 1]
    return result_rows.astype(jnp.bfloat16)


def dot32(a, b):
    return lax.dot_general(
        a, b, (((1,), (0,)), ((), ())), preferred_element_type=jnp.float32
    )


def dot32_t(a, b):
    return lax.dot_general(
        a, b, (((1,), (1,)), ((), ())), preferred_element_type=jnp.float32
    )


bf = jnp.bfloat16
VMEM = pl.BlockSpec(memory_space=pltpu.VMEM)
SMEM = pl.BlockSpec(memory_space=pltpu.SMEM)
ANY = pl.BlockSpec(memory_space=pl.ANY)


def call(kernel, outs, out_specs, in_specs, scratch=(), flops=0, moved=0):
    return pl.pallas_call(
        kernel,
        out_shape=outs,
        in_specs=in_specs,
        out_specs=out_specs,
        scratch_shapes=list(scratch),
        compiler_params=pltpu.CompilerParams(vmem_limit_bytes=40 * 1024 * 1024),
        cost_estimate=pl.CostEstimate(flops=flops, bytes_accessed=moved, transcendentals=0),
    )


def shape(*dims, dtype=bf):
    return jax.ShapeDtypeStruct(dims, dtype)


def lanes(index, size):
    return pl.ds(pl.multiple_of(index * size, 128), size)


def copy_kernel(first, count, weights, out, sems):
    copies = [
        pltpu.make_async_copy(weights.at[m, pl.ds(first, count)], out.at[m], sems.at[m])
        for m in (0, 1)
    ]
    for copy in copies:
        copy.start()
    for copy in copies:
        copy.wait()


def sign_pieces(bits, u, team):
    piece = bits.shape[0] // team
    parts = [bits[pl.ds(pl.multiple_of((u ^ r) * piece, 8), piece), :] for r in range(team)]
    return [(2 * part - 1).astype(jnp.float32) for part in parts]


def prepare_kernel(team, place, tokens, in_bits, sign_bits, *blocks):
    z = place[0]
    wide = tokens.shape[1] // len(blocks)
    signs = [part.astype(bf) for part in sign_pieces(sign_bits.at[2], place[2], team)]
    for k, block in enumerate(blocks):
        cut = lanes(z ^ k, wide)
        plain = tokens[:, cut]
        sign = (2 * in_bits[:, cut] - 1).astype(jnp.float32)
        block[0] = plain
        block[1] = (plain.astype(jnp.float32) * sign).astype(bf)
        for r in range(team):
            block[2 + r] = signs[r]


def rest_kernel(team, place, sign_bits, mix_bits, weights, query_a, query_b, signs, mix, sems):
    copies = [
        pltpu.make_async_copy(weights.at[m, 0], out, sems.at[m])
        for m, out in ((0, query_a), (1, query_b))
    ]
    for copy in copies:
        copy.start()
    for part in (0, 1):
        pieces = sign_pieces(sign_bits.at[part], place[2], team)
        signs[part] = jnp.concatenate(pieces, axis=0).astype(bf)
    mix[...] = jnp.concatenate(sign_pieces(mix_bits, place[2], team), axis=0).astype(bf)
    for copy in copies:
        copy.wait()


def stack_kernel(*refs):
    for k, ref in enumerate(refs[:-1]):
        refs[-1][k] = ref[: refs[-1].shape[1]]


def pair_kernel(own, taken, out):
    out[0] = own[...]
    out[1] = taken[...]


def rows_kernel(own, taken, rows):
    depth, kinds, piece = own.shape[1:4]
    for m in range(kinds):
        for j in range(depth):
            parts = [ref[y, j, m].astype(jnp.float32) for y in (0, 1) for ref in (own, taken)]
            at = j * 4 * piece
            rows[m, at : at + 4 * piece] = jnp.concatenate(parts, axis=0).astype(bf)


def sum_kernel(total, taken, out):
    out[...] = (total[...] + taken[...].astype(jnp.float32)).astype(bf)


def project_kernel(part, size, place, rows, weights, partner_0, partner_1, *refs):
    held, total, sems = refs[-3:]
    z, x = place[0], place[1]
    slab = weights.shape[2]
    partner = (partner_0, partner_1)
    if part:
        partner = (partner_0.at[0, part - 1], partner_0.at[1, part - 1])
    own = pl.ds(pl.multiple_of(x * slab, 64), slab)
    other = pl.ds(pl.multiple_of((1 - x) * slab, 64), slab)
    copies = []
    for m in (0, 1):
        copies.append(
            pltpu.make_async_copy(weights.at[m, part], held.at[m, own], sems.at[m, 0])
        )
        copies.append(pltpu.make_async_copy(partner[m], held.at[m, other], sems.at[m, 1]))
    for copy in copies:
        copy.start()
    for copy in copies:
        copy.wait()
    depth = rows.shape[1] // size
    outs = refs[depth:-3]

    def sign(j):
        if part < 2:
            return refs[j][part].astype(jnp.float32)
        pieces = [refs[j][r] for r in range(2, refs[j].shape[0])]
        return jnp.concatenate([piece.astype(jnp.float32) for piece in pieces], axis=0)

    total[...] = dot32(rows[1], held[1])
    plain = dot32(rows[0], held[0])
    for j in range(depth):
        cut = slice(j * size, (j + 1) * size)
        total[cut] = plain[cut] + sign(j) * total[cut]

    def block(j, head):
        return total[j * size : (j + 1) * size, lanes(head, HEAD)]

    def main(target, start, k):
        for j in range(depth):
            at = start + (j ^ k) * size
            target[at : at + size] = block(j, z ^ k).astype(target.dtype)

    def rest(target, start, j):
        target[start : start + size] = block(j, depth).astype(target.dtype)

    half = depth * size
    if part:
        send, keep_own, keep_two = outs
        main(send, 0, 1)
        main(send, half, 3)
        for j in range(depth):
            rest(send, 2 * half + (j ^ 1) * size, j)
            rest(keep_own, half + j * size, j)
        main(keep_own, 0, 0)
        main(keep_two, 0, 2)
    else:
        for k in range(depth):
            main(outs[k], 0, k)
            rest(outs[k], half, k)


def middle_kernel(size, keep_own, keep_two, taken, send, total):
    half = keep_two.shape[0]
    total[:half] = keep_own[:half] + taken[:half].astype(jnp.float32)
    send[:half] = (keep_two[...] + taken[half : 2 * half].astype(jnp.float32)).astype(bf)
    for j in range(half // size):
        cut = slice(half + j * size, half + (j + 1) * size)
        got = taken[half + cut.start : half + cut.stop].astype(jnp.float32)
        value = keep_own[cut] + got
        total[cut] = value
        at = half + (j ^ 2) * size
        send[at : at + size] = value.astype(bf)


def norm_rows(values, gain_row):
    wide = values.astype(jnp.float32)
    inverse_rms = lax.rsqrt(jnp.mean(wide * wide, axis=-1, keepdims=True) + epsilon)
    return (wide * inverse_rms * gain_row).astype(bf)


def key_kernel(half, place, total, taken, gain, keys):
    keep = (total[...] + taken[...].astype(jnp.float32)).astype(bf)
    heads = gain.shape[0]
    keys[:half] = norm_rows(keep[:half], gain[pl.ds(place[0], 1), :])
    keys[half:] = norm_rows(keep[half:], gain[heads - 1 : heads, :])


def attend_kernel(
    half, place, total, taken_1, taken_2, taken_3, gain, keys_a, keys_b, values_a, values_b, out
):
    keep = total[...]
    for taken in (taken_1, taken_2, taken_3):
        keep = keep + taken[...].astype(jnp.float32)
    keep = keep.astype(bf)
    heads = gain.shape[0]

    def attend(queries, cut):
        score_scale = 1.0 / math.sqrt(HEAD)
        totals, sums = 0.0, 0.0
        for keys, values in ((keys_a, values_a), (keys_b, values_b)):
            scores = dot32_t(queries, keys[cut]) * score_scale
            weights = jnp.exp(scores).astype(bf)
            totals = totals + jnp.sum(weights.astype(jnp.float32), axis=1, keepdims=True)
            sums = sums + dot32(weights, values[cut])
        return (sums / totals).astype(bf)

    first = norm_rows(keep[:half], gain[pl.ds(place[0], 1), :])
    out[:half] = attend(first, slice(0, half))
    last = norm_rows(keep[half:], gain[heads - 1 : heads, :])
    out[half:] = attend(last, slice(half, 2 * half))


def final_kernel(place, bits, *refs):
    out = refs[-1]
    for k, block in enumerate(refs[:-1]):
        cut = lanes(place[0] ^ k, block.shape[2])
        sign = (2 * bits[:, cut] - 1).astype(jnp.float32)
        out[:, cut] = (block[0].astype(jnp.float32) + sign * block[1].astype(jnp.float32)).astype(bf)


def stationary_plan(
    tokens, in_bits, qkv_weights, qkv_bits, gain_query, gain_key, out_weights, mix_bits, out_bits
):
    groups = lax.axis_size("blk")
    team = lax.axis_size("uly")
    depth = groups // 2
    z = lax.axis_index("blk") // 2
    x = lax.axis_index("blk") % 2
    u = lax.axis_index("uly")
    own_rows, width = tokens.shape
    slab = qkv_weights.shape[2]
    columns = qkv_weights.shape[3]
    size = own_rows * team
    heads = columns // HEAD
    half = depth * size
    steps = range(depth)
    f32 = jnp.float32
    place = jnp.stack([z, x, u]).astype(jnp.int32)

    def swap_x(value):
        return lax.ppermute(value, "blk", [(i, i ^ 1) for i in range(groups)])

    def swap_z(value, step):
        return lax.ppermute(value, "blk", [(i, i ^ (2 * step)) for i in range(groups)])

    def swap_u(value, bit):
        return lax.ppermute(value, "uly", [(i, i ^ bit) for i in range(team)])

    def after(value, *earlier):
        return lax.optimization_barrier((value,) + earlier)[0]

    early = call(
        functools.partial(copy_kernel, 1, 2),
        shape(2, 2, slab, columns), ANY, [ANY], [pltpu.SemaphoreType.DMA((2,))],
    )(qkv_weights)
    partner_early = swap_x(early)

    sign_bits = jnp.transpose(qkv_bits, (1, 0, 2))
    blocks = call(
        functools.partial(prepare_kernel, team),
        [shape(2 + team, own_rows, 2 * slab)] * depth, [VMEM] * depth, [SMEM] + [VMEM] * 3,
    )(place, after(tokens, early), in_bits, sign_bits)
    got = [blocks[0]] + [swap_z(blocks[k], k) for k in steps if k]
    query_a, query_b, sign_pair, mix_own = call(
        functools.partial(rest_kernel, team),
        [shape(slab, columns), shape(slab, columns), shape(2, size, columns), shape(size, columns)],
        [ANY, ANY, VMEM, VMEM],
        [SMEM, VMEM, VMEM, ANY],
        [pltpu.SemaphoreType.DMA((2,))],
    )(place, after(sign_bits, blocks[0]), mix_bits, qkv_weights)
    sent_pair = after(sign_pair, *got[1:])
    pairs = [sign_pair] + [swap_z(sent_pair, k) for k in steps if k]
    signs = {2: got, 1: pairs, 0: pairs}

    held_shape = (depth, 2, own_rows, 2 * slab)
    held = call(stack_kernel, shape(*held_shape), VMEM, [VMEM] * depth)(*got)
    held = call(pair_kernel, shape(2, *held_shape), VMEM, [VMEM] * 2)(held, swap_u(held, 2))
    rows = call(rows_kernel, shape(2, half, 2 * slab), VMEM, [VMEM] * 2)(held, swap_u(held, 1))

    query_a = swap_x(after(query_a, partner_early, pairs[1]))
    query_b = swap_x(after(query_b, query_a))
    partner = {2: [partner_early] * 2, 1: [partner_early] * 2, 0: [query_a, query_b]}

    def project(part, rows, outs):
        return call(
            functools.partial(project_kernel, part, size),
            outs,
            [VMEM] * len(outs),
            [SMEM, VMEM, ANY, ANY, ANY] + [VMEM] * len(signs[part]),
            [
                pltpu.VMEM((2, 2 * slab, columns), bf),
                pltpu.VMEM((half, columns), f32),
                pltpu.SemaphoreType.DMA((2, 2)),
            ],
        )(place, rows, qkv_weights, *partner[part], *signs[part])

    two_step = [
        shape(3 * half, HEAD), shape(2 * half, HEAD, dtype=f32), shape(half, HEAD, dtype=f32)
    ]

    def middle(keep_own, keep_two, taken):
        return call(
            functools.partial(middle_kernel, size),
            [shape(2 * half, HEAD), shape(2 * half, HEAD, dtype=f32)],
            [VMEM] * 2,
            [VMEM] * 3,
        )(keep_own, keep_two, taken)

    value_send, keep_own, keep_two = project(2, rows, two_step)
    key_send, key_own, key_two = project(1, after(rows, value_send), two_step)
    taken = after(swap_z(value_send, 1), key_send, query_a)
    send, value_total = middle(keep_own, keep_two, taken)
    value_last = swap_z(send, 2)
    taken = after(swap_z(key_send, 1), value_total, query_b)
    send, key_total = middle(key_own, key_two, taken)
    key_last = swap_z(send, 2)
    own, *sends = project(
        0,
        after(rows, key_total),
        [shape(half + size, HEAD, dtype=f32)] + [shape(half + size, HEAD)] * 3,
    )
    taken_q = [swap_z(sends[k - 1], k) for k in steps if k]
    values = call(sum_kernel, shape(2 * half, HEAD), VMEM, [VMEM] * 2)(
        value_total, after(value_last, own)
    )
    values_partner = swap_x(values)
    keys = call(
        functools.partial(key_kernel, half), shape(2 * half, HEAD), VMEM, [SMEM] + [VMEM] * 3
    )(place, key_total, after(key_last, values, taken_q[0]), gain_key.reshape(heads, HEAD))
    keys_partner = swap_x(keys)
    mix_two = swap_z(after(mix_own, taken_q[1]), 2)
    mix_13 = swap_z(
        call(pair_kernel, shape(2, size, columns), VMEM, [VMEM] * 2)(mix_own, mix_two), 1
    )
    out_t = jnp.transpose(out_weights, (0, 2, 1))
    out_partner = swap_x(after(out_t, keys, taken_q[1]))

    done = call(
        functools.partial(attend_kernel, half),
        shape(half + size, HEAD),
        VMEM,
        [SMEM] + [VMEM] * 9,
    )(
        place, own, *taken_q,
        gain_query.reshape(heads, HEAD), keys, keys_partner, values, values_partner,
    )

    by_head, last_head = [], []
    for k in steps:
        block = swap_z(done, k) if k else done
        main = block[:half].reshape(depth, size, HEAD)
        by_head.append(jnp.concatenate([main[j ^ k] for j in steps], axis=0))
        last_head.append(block[half:])
    attended = jnp.concatenate(by_head + [jnp.concatenate(last_head, axis=0)], axis=1)

    def relative(value, axis):
        parts = [
            lax.dynamic_slice_in_dim(value, (z ^ k) * HEAD, HEAD, axis) for k in steps
        ] + [lax.slice_in_dim(value, depth * HEAD, heads * HEAD, axis=axis)]
        return jnp.concatenate(parts, axis=axis)

    mix = relative(jnp.concatenate([mix_own, mix_13[0], mix_two, mix_13[1]], axis=0), 1)
    attended_flipped = attended * mix
    first = jnp.where(x == 0, out_t, out_partner)
    second = jnp.where(x == 0, out_partner, out_t)
    out_full = relative(jnp.concatenate([first, second], axis=1), 2)
    partial = jnp.stack(
        [dot32_t(attended, out_full[0]), dot32_t(attended_flipped, out_full[1])]
    ).astype(bf)
    partial = partial.reshape(2, depth, team, own_rows, 2 * slab)
    summed = partial[:, :, 0::2].astype(f32) + swap_u(partial[:, :, 1::2], 1).astype(f32)
    summed = (summed[:, :, 0] + swap_u(summed[:, :, 1].astype(bf), 2).astype(f32)).astype(bf)
    final = [summed[:, 0]] + [swap_z(summed[:, k], k) for k in steps if k]
    own_bits = lax.dynamic_slice_in_dim(out_bits, u * own_rows, own_rows, 0)
    return call(
        final_kernel, shape(own_rows, width), VMEM, [SMEM] + [VMEM] * (1 + depth)
    )(place, own_bits, *final)


def body(*arrays):
    heads = arrays[2].shape[3] // HEAD
    depth = lax.axis_size("blk") // 2
    if depth == heads - 1 and depth == 4 and lax.axis_size("uly") == 4:
        return stationary_plan(*arrays)
    return gather_plan(*arrays)


def solution(mesh):
    return jax.shard_map(
        body,
        mesh=mesh,
        in_specs=(
            P(("blk", "uly"), None),
            P(("blk", "uly"), None),
            P(None, None, "blk", "uly"),
            P("blk", None, "uly"),
            P("uly"),
            P("uly"),
            P(None, "uly", "blk"),
            P("blk", "uly"),
            P("blk", None),
        ),
        out_specs=P(("blk", "uly"), None),
        check_vma=False,
    )
```

profile of v0, /device:TPU:0, one launch (start us, length us, event | category | flops | bytes accessed | tf_op | source)
XLA Modules:
  0.0 152.9 jit_solution(13981939288529673401)
XLA Ops:
  0.0 1.8 %copy-done.1 = bf16[2,3,320,640]{3,2,1,0:T(8,128)(2,1)S(1)} copy-done((bf16[2,3,320,640]{3,2,1,0:T(8,128)(2,1)S(1)}, bf16[2,3,320,640]{3,2,1,0:T(8,128)(2,1)}, u32[]{:S(2)}) %copy-start.1) | copy-done | bytes 2457624
  1.8 1.2 shard_map.91
  3.0 3.0 %collective-permute-start.5 = (bf16[2,2,320,640]{3,2,1,0:T(8,128)(2,1)}, bf16[2,2,320,640]{3,2,1,0:T(8,128)(2,1)}, u32[]{:S(2)}, u32[]{:S(2)}) collective-permute-start(bf16[2,2,320,640]{3,2,1,0:T(8,128)(2,1)} %shard_map.91), channel_id=1, source_target_pairs={{0,4},{4,0},{8,12},{12,8},{16,20},{20,16},{24,28},{28,24},{1,5},{5... | collective-permute-start | bytes 4915208 | tf_op jit(solution)/shard_map/ppermute | solution.py:349
  6.1 1.1 copy-done.3
  7.2 0.9 copy-done.5
  9.7 1.6 %collective-permute-start = (bf16[6,24,640]{2,1,0:T(8,128)(2,1)S(1)}, bf16[6,24,640]{2,1,0:T(8,128)(2,1)S(1)}, u32[]{:S(2)}, u32[]{:S(2)}) collective-permute-start(bf16[6,24,640]{2,1,0:T(8,128)(2,1)S(1)} %get-tuple-element.42), channel_id=1, source_target_pairs={{0,8},{4,12},{8,0},{12,4},{16,24},{20,28},{24,16},{28,20},{1,9},{5... | collective-permute-start | bytes 552968 | tf_op jit(solution)/shard_map/ppermute | solution.py:352
  11.3 2.6 %collective-permute-start.1 = (bf16[6,24,640]{2,1,0:T(8,128)(2,1)S(1)}, bf16[6,24,640]{2,1,0:T(8,128)(2,1)S(1)}, u32[]{:S(2)}, u32[]{:S(2)}) collective-permute-start(bf16[6,24,640]{2,1,0:T(8,128)(2,1)S(1)} %get-tuple-element.43), channel_id=1, source_target_pairs={{0,16},{4,20},{8,24},{12,28},{16,0},{20,4},{24,8},{28,12},{1,17},{... | collective-permute-start | bytes 552968 | tf_op jit(solution)/shard_map/ppermute | solution.py:352
  14.1 1.1 copy-done.4
  15.3 0.9 copy-done.6
  16.2 1.7 %shard_map.97 = (bf16[320,640]{1,0:T(8,128)(2,1)S(1)}, bf16[320,640]{1,0:T(8,128)(2,1)S(1)}, bf16[2,96,640]{2,1,0:T(8,128)(2,1)S(1)}, bf16[96,640]{1,0:T(8,128)(2,1)}) custom-call(s32[3]{0:T(128)S(1)} %pad_add_fusion.place, s32[3,96,640]{2,1,0:T(8,128)S(1)} %bitcast.55, s32[96,640]{1,0:T(8,128)S(1)} %copy-done.6, bf16[2,3,320,640]{3,2,1,0:T(8,128)(2,1)S(1)} %copy-done.2), custom_call_target="tpu_custom_call" | custom-call | tf_op jit(solution)/shard_map/pallas_call | solution.py:372
  18.7 9.0 %collective-permute-done.1.refs_2_ = bf16[6,24,640]{2,1,0:T(8,128)(2,1)S(1)} collective-permute-done((bf16[6,24,640]{2,1,0:T(8,128)(2,1)S(1)}, bf16[6,24,640]{2,1,0:T(8,128)(2,1)S(1)}, u32[]{:S(2)}, u32[]{:S(2)}) %collective-permute-start.1) | collective-permute-done | bytes 184352 | tf_op jit(solution)/shard_map/ppermute | solution.py:352
  27.7 2.8 %collective-permute-start.6 = (bf16[2,96,640]{2,1,0:T(8,128)(2,1)S(1)}, bf16[2,96,640]{2,1,0:T(8,128)(2,1)S(1)}, u32[]{:S(2)}, u32[]{:S(2)}) collective-permute-start(bf16[2,96,640]{2,1,0:T(8,128)(2,1)S(1)} %get-tuple-element.49.refs_0_), channel_id=1, source_target_pairs={{0,8},{4,12},{8,0},{12,4},{16,24},{20,28},{24,16},{28,20},{1,9},{5... | collective-permute-start | bytes 737288 | tf_op jit(solution)/shard_map/ppermute | solution.py:352
  30.5 1.6 %collective-permute-start.3 = (bf16[4,2,24,640]{3,2,1,0:T(8,128)(2,1)S(1)}, bf16[4,2,24,640]{3,2,1,0:T(8,128)(2,1)S(1)}, u32[]{:S(2)}, u32[]{:S(2)}) collective-permute-start(bf16[4,2,24,640]{3,2,1,0:T(8,128)(2,1)S(1)} %shard_map.93.own), channel_id=1, source_target_pairs={{0,2},{1,3},{2,0},{3,1},{4,6},{5,7},{6,4},{7,5},{8,10},{9,11},{10,... | collective-permute-start | bytes 737288 | tf_op jit(solution)/shard_map/ppermute | solution.py:355
  32.1 3.0 %collective-permute-done.6.refs_1_ = bf16[2,96,640]{2,1,0:T(8,128)(2,1)S(1)} collective-permute-done((bf16[2,96,640]{2,1,0:T(8,128)(2,1)S(1)}, bf16[2,96,640]{2,1,0:T(8,128)(2,1)S(1)}, u32[]{:S(2)}, u32[]{:S(2)}) %collective-permute-start.6) | collective-permute-done | bytes 245792 | tf_op jit(solution)/shard_map/ppermute | solution.py:352
  35.1 7.0 %collective-permute-done.5.partner_0.partner_1 = bf16[2,2,320,640]{3,2,1,0:T(8,128)(2,1)} collective-permute-done((bf16[2,2,320,640]{3,2,1,0:T(8,128)(2,1)}, bf16[2,2,320,640]{3,2,1,0:T(8,128)(2,1)}, u32[]{:S(2)}, u32[]{:S(2)}) %collective-permute-start.5) | collective-permute-done | bytes 1638432 | tf_op jit(solution)/shard_map/ppermute | solution.py:349
  42.1 1.7 %collective-permute-start.11 = (bf16[320,640]{1,0:T(8,128)(2,1)S(1)}, bf16[320,640]{1,0:T(8,128)(2,1)S(1)}, u32[]{:S(2)}, u32[]{:S(2)}) collective-permute-start(bf16[320,640]{1,0:T(8,128)(2,1)S(1)} %get-tuple-element.56), channel_id=1, source_target_pairs={{0,4},{4,0},{8,12},{12,8},{16,20},{20,16},{24,28},{28,24},{1,5},{5... | collective-permute-start | bytes 1228808 | tf_op jit(solution)/shard_map/ppermute | solution.py:349
  44.0 2.7 %collective-permute-start.7 = (bf16[2,96,640]{2,1,0:T(8,128)(2,1)S(1)}, bf16[2,96,640]{2,1,0:T(8,128)(2,1)S(1)}, u32[]{:S(2)}, u32[]{:S(2)}) collective-permute-start(bf16[2,96,640]{2,1,0:T(8,128)(2,1)S(1)} %get-tuple-element.49.refs_0_), channel_id=1, source_target_pairs={{0,16},{4,20},{8,24},{12,28},{16,0},{20,4},{24,8},{28,12},{1,17},{... | collective-permute-start | bytes 737288 | tf_op jit(solution)/shard_map/ppermute | solution.py:352
  46.6 1.3 collective-permute-start.8
  48.0 4.8 %collective-permute-done.11.partner_0 = bf16[320,640]{1,0:T(8,128)(2,1)S(1)} collective-permute-done((bf16[320,640]{1,0:T(8,128)(2,1)S(1)}, bf16[320,640]{1,0:T(8,128)(2,1)S(1)}, u32[]{:S(2)}, u32[]{:S(2)}) %collective-permute-start.11) | collective-permute-done | bytes 409632 | tf_op jit(solution)/shard_map/ppermute | solution.py:349
  52.8 1.4 collective-permute-start.12
  54.3 3.1 %shard_map.96 = (bf16[1152,128]{1,0:T(8,128)(2,1)S(1)}, f32[768,128]{1,0:T(8,128)S(1)}, f32[384,128]{1,0:T(8,128)S(1)}) custom-call(s32[3]{0:T(128)S(1)} %pad_add_fusion.place, bf16[2,384,640]{2,1,0:T(8,128)(2,1)S(1)} %shard_map.95.rows, bf16[2,3,320,640]{3,2,1,0:T(8,128)(2,1)S(1)} %copy-done.2, ...), custom_call_target="tpu_custom_call" | custom-call | tf_op jit(solution)/shard_map/pallas_call | solution.py:393
  57.4 1.6 %collective-permute-start.10 = (bf16[1152,128]{1,0:T(8,128)(2,1)S(1)}, bf16[1152,128]{1,0:T(8,128)(2,1)S(1)}, u32[]{:S(2)}, u32[]{:S(2)}) collective-permute-start(bf16[1152,128]{1,0:T(8,128)(2,1)S(1)} %get-tuple-element.45), channel_id=1, source_target_pairs={{0,8},{4,12},{8,0},{12,4},{16,24},{20,28},{24,16},{28,20},{1,9},{5... | collective-permute-start | bytes 884744 | tf_op jit(solution)/shard_map/ppermute | solution.py:352
  59.1 5.2 %collective-permute-done.7.refs_2_ = bf16[2,96,640]{2,1,0:T(8,128)(2,1)S(1)} collective-permute-done((bf16[2,96,640]{2,1,0:T(8,128)(2,1)S(1)}, bf16[2,96,640]{2,1,0:T(8,128)(2,1)S(1)}, u32[]{:S(2)}, u32[]{:S(2)}) %collective-permute-start.7) | collective-permute-done | bytes 245792 | tf_op jit(solution)/shard_map/ppermute | solution.py:352
  64.3 3.1 %shard_map.98 = (bf16[1152,128]{1,0:T(8,128)(2,1)S(1)}, f32[768,128]{1,0:T(8,128)S(1)}, f32[384,128]{1,0:T(8,128)S(1)}) custom-call(s32[3]{0:T(128)S(1)} %pad_add_fusion.place, bf16[2,384,640]{2,1,0:T(8,128)(2,1)S(1)} %shard_map.95.rows, bf16[2,3,320,640]{3,2,1,0:T(8,128)(2,1)S(1)} %copy-done.2, ...), custom_call_target="tpu_custom_call" | custom-call | tf_op jit(solution)/shard_map/pallas_call | solution.py:393
  67.4 5.6 %collective-permute-start.9 = (bf16[1152,128]{1,0:T(8,128)(2,1)S(1)}, bf16[1152,128]{1,0:T(8,128)(2,1)S(1)}, u32[]{:S(2)}, u32[]{:S(2)}) collective-permute-start(bf16[1152,128]{1,0:T(8,128)(2,1)S(1)} %get-tuple-element.52), channel_id=1, source_target_pairs={{0,8},{4,12},{8,0},{12,4},{16,24},{20,28},{24,16},{28,20},{1,9},{5... | collective-permute-start | bytes 884744 | tf_op jit(solution)/shard_map/ppermute | solution.py:352
  73.0 2.0 %collective-permute-start.17 = (bf16[768,128]{1,0:T(8,128)(2,1)S(1)}, bf16[768,128]{1,0:T(8,128)(2,1)S(1)}, u32[]{:S(2)}, u32[]{:S(2)}) collective-permute-start(bf16[768,128]{1,0:T(8,128)(2,1)S(1)} %get-tuple-element.69), channel_id=1, source_target_pairs={{0,16},{4,20},{8,24},{12,28},{16,0},{20,4},{24,8},{28,12},{1,17},{... | collective-permute-start | bytes 589832 | tf_op jit(solution)/shard_map/ppermute | solution.py:352
  75.0 9.4 %collective-permute-done.9.taken = bf16[1152,128]{1,0:T(8,128)(2,1)S(1)} collective-permute-done((bf16[1152,128]{1,0:T(8,128)(2,1)S(1)}, bf16[1152,128]{1,0:T(8,128)(2,1)S(1)}, u32[]{:S(2)}, u32[]{:S(2)}) %collective-permute-start.9) | collective-permute-done | bytes 294944 | tf_op jit(solution)/shard_map/ppermute | solution.py:352
  84.5 1.4 collective-permute-start.16
  85.8 3.2 %shard_map.101 = (f32[480,128]{1,0:T(8,128)S(1)}, bf16[480,128]{1,0:T(8,128)(2,1)S(1)}, bf16[480,128]{1,0:T(8,128)(2,1)S(1)}, bf16[480,128]{1,0:T(8,128)(2,1)}) custom-call(s32[3]{0:T(128)S(1)} %pad_add_fusion.place, bf16[2,384,640]{2,1,0:T(8,128)(2,1)S(1)} %shard_map.95.rows, bf16[2,3,320,640]{3,2,1,0:T(8,128)(2,1)S(1)} %copy-done.2, ...), custom_call_target="tpu_custom_call" | custom-call | tf_op jit(solution)/shard_map/pallas_call | solution.py:393
  89.0 2.5 %collective-permute-start.13 = (bf16[480,128]{1,0:T(8,128)(2,1)S(1)}, bf16[480,128]{1,0:T(8,128)(2,1)S(1)}, u32[]{:S(2)}, u32[]{:S(2)}) collective-permute-start(bf16[480,128]{1,0:T(8,128)(2,1)S(1)} %get-tuple-element.65), channel_id=1, source_target_pairs={{0,8},{4,12},{8,0},{12,4},{16,24},{20,28},{24,16},{28,20},{1,9},{5... | collective-permute-start | bytes 368648 | tf_op jit(solution)/shard_map/ppermute | solution.py:352
  92.3 4.7 %collective-permute-done.13.taken_1 = bf16[480,128]{1,0:T(8,128)(2,1)S(1)} collective-permute-done((bf16[480,128]{1,0:T(8,128)(2,1)S(1)}, bf16[480,128]{1,0:T(8,128)(2,1)S(1)}, u32[]{:S(2)}, u32[]{:S(2)}) %collective-permute-start.13) | collective-permute-done | bytes 122912 | tf_op jit(solution)/shard_map/ppermute | solution.py:352
  97.0 2.5 %collective-permute-done.16.taken = bf16[768,128]{1,0:T(8,128)(2,1)S(1)} collective-permute-done((bf16[768,128]{1,0:T(8,128)(2,1)S(1)}, bf16[768,128]{1,0:T(8,128)(2,1)S(1)}, u32[]{:S(2)}, u32[]{:S(2)}) %collective-permute-start.16) | collective-permute-done | bytes 196640 | tf_op jit(solution)/shard_map/ppermute | solution.py:352
  101.3 2.2 %collective-permute-start.15 = (bf16[480,128]{1,0:T(8,128)(2,1)}, bf16[480,128]{1,0:T(8,128)(2,1)S(1)}, u32[]{:S(2)}, u32[]{:S(2)}) collective-permute-start(bf16[480,128]{1,0:T(8,128)(2,1)} %get-tuple-element.67), channel_id=1, source_target_pairs={{0,24},{4,28},{8,16},{12,20},{16,8},{20,12},{24,0},{28,4},{1,25},{... | collective-permute-start | bytes 368648 | tf_op jit(solution)/shard_map/ppermute | solution.py:352
  104.1 8.5 %collective-permute-done.24.taken = bf16[96,640]{1,0:T(8,128)(2,1)S(1)} collective-permute-done((bf16[96,640]{1,0:T(8,128)(2,1)}, bf16[96,640]{1,0:T(8,128)(2,1)S(1)}, u32[]{:S(2)}, u32[]{:S(2)}) %collective-permute-start.24) | collective-permute-done | bytes 122912 | tf_op jit(solution)/shard_map/ppermute | solution.py:352
  113.7 0.9 copy-done.8
  114.6 1.4 shard_map.104
  116.0 2.1 %collective-permute-start.20 = (bf16[480,128]{1,0:T(8,128)(2,1)S(1)}, bf16[480,128]{1,0:T(8,128)(2,1)S(1)}, u32[]{:S(2)}, u32[]{:S(2)}) collective-permute-start(bf16[480,128]{1,0:T(8,128)(2,1)S(1)} %shard_map.104), channel_id=1, source_target_pairs={{0,8},{4,12},{8,0},{12,4},{16,24},{20,28},{24,16},{28,20},{1,9},{5... | collective-permute-start | bytes 368648 | tf_op jit(solution)/shard_map/ppermute | solution.py:352
  118.1 2.4 %collective-permute-start.22 = (bf16[480,128]{1,0:T(8,128)(2,1)S(1)}, bf16[480,128]{1,0:T(8,128)(2,1)S(1)}, u32[]{:S(2)}, u32[]{:S(2)}) collective-permute-start(bf16[480,128]{1,0:T(8,128)(2,1)S(1)} %shard_map.104), channel_id=1, source_target_pairs={{0,24},{4,28},{8,16},{12,20},{16,8},{20,12},{24,0},{28,4},{1,25},{... | collective-permute-start | bytes 368648 | tf_op jit(solution)/shard_map/ppermute | solution.py:352
  120.6 3.2 %collective-permute-done.25 = bf16[2,96,640]{2,1,0:T(8,128)(2,1)S(1)} collective-permute-done((bf16[2,96,640]{2,1,0:T(8,128)(2,1)S(1)}, bf16[2,96,640]{2,1,0:T(8,128)(2,1)S(1)}, u32[]{:S(2)}, u32[]{:S(2)}) %collective-permute-start.25) | collective-permute-done | bytes 245792 | tf_op jit(solution)/shard_map/ppermute | solution.py:352
  123.9 0.9 pad_maximum_fusion.1
  125.4 4.8 %collective-permute-done.21 = bf16[480,128]{1,0:T(8,128)(2,1)S(1)} collective-permute-done((bf16[480,128]{1,0:T(8,128)(2,1)S(1)}, bf16[480,128]{1,0:T(8,128)(2,1)S(1)}, u32[]{:S(2)}, u32[]{:S(2)}) %collective-permute-start.21) | collective-permute-done | bytes 122912 | tf_op jit(solution)/shard_map/ppermute | solution.py:352
  132.8 1.9 %collective-permute-done.26 = bf16[2,4,2,24,640]{4,3,0,1,2:T(8,128)(2,1)S(1)} collective-permute-done((bf16[2,4,2,24,640]{4,3,0,1,2:T(8,128)(2,1)S(1)}, bf16[2,4,2,24,640]{4,3,0,1,2:T(8,128)(2,1)S(1)}, u32[]{:S(2)}, u32[]{:S(2)}) %collective-permute-start.26) | collective-permute-done | bytes 491552 | tf_op jit(solution)/shard_map/ppermute | solution.py:355
  134.8 1.6 %collective-permute-start.27 = (bf16[2,4,24,640]{3,2,0,1:T(8,128)(2,1)S(1)}, bf16[2,4,24,640]{3,2,0,1:T(8,128)(2,1)S(1)}, u32[]{:S(2)}, u32[]{:S(2)}) collective-permute-start(bf16[2,4,24,640]{3,2,0,1:T(8,128)(2,1)S(1)} %fusion.15), channel_id=1, source_target_pairs={{0,2},{1,3},{2,0},{3,1},{4,6},{5,7},{6,4},{7,5},{8,10},{9,11},{10,... | collective-permute-start | bytes 737288 | tf_op jit(solution)/shard_map/ppermute | solution.py:355
  136.4 6.5 %collective-permute-done.27 = bf16[2,4,24,640]{3,2,0,1:T(8,128)(2,1)S(1)} collective-permute-done((bf16[2,4,24,640]{3,2,0,1:T(8,128)(2,1)S(1)}, bf16[2,4,24,640]{3,2,0,1:T(8,128)(2,1)S(1)}, u32[]{:S(2)}, u32[]{:S(2)}) %collective-permute-start.27) | collective-permute-done | bytes 245792 | tf_op jit(solution)/shard_map/ppermute | solution.py:355
  142.9 1.8 %collective-permute-start.28 = (bf16[2,24,640]{2,1,0:T(8,128)(2,1)S(1)}, bf16[2,24,640]{2,1,0:T(8,128)(2,1)S(1)}, u32[]{:S(2)}, u32[]{:S(2)}) collective-permute-start(bf16[2,24,640]{2,1,0:T(8,128)(2,1)S(1)} %get-tuple-element.84), channel_id=1, source_target_pairs={{0,8},{4,12},{8,0},{12,4},{16,24},{20,28},{24,16},{28,20},{1,9},{5... | collective-permute-start | bytes 184328 | tf_op jit(solution)/shard_map/ppermute | solution.py:352
  144.9 2.5 %collective-permute-start.30 = (bf16[2,24,640]{2,1,0:T(8,128)(2,1)S(1)}, bf16[2,24,640]{2,1,0:T(8,128)(2,1)S(1)}, u32[]{:S(2)}, u32[]{:S(2)}) collective-permute-start(bf16[2,24,640]{2,1,0:T(8,128)(2,1)S(1)} %get-tuple-element.82), channel_id=1, source_target_pairs={{0,24},{4,28},{8,16},{12,20},{16,8},{20,12},{24,0},{28,4},{1,25},{... | collective-permute-start | bytes 184328 | tf_op jit(solution)/shard_map/ppermute | solution.py:352
  147.4 4.2 %collective-permute-done.29.refs_2_ = bf16[2,24,640]{2,1,0:T(8,128)(2,1)S(1)} collective-permute-done((bf16[2,24,640]{2,1,0:T(8,128)(2,1)S(1)}, bf16[2,24,640]{2,1,0:T(8,128)(2,1)S(1)}, u32[]{:S(2)}, u32[]{:S(2)}) %collective-permute-start.29) | collective-permute-done | bytes 61472 | tf_op jit(solution)/shard_map/ppermute | solution.py:352
  151.7 1.3 shard_map.106
  (94 shorter events, 10.4 us)
Async XLA Ops:
  0.0 147.4 %copy-start = (s32[96,2560]{1,0:T(8,128)S(1)}, s32[96,2560]{1,0:T(8,128)}, u32[]{:S(2)}) copy-start(s32[96,2560]{1,0:T(8,128)} %param.17) | copy-start | bytes 2949124
  0.0 1.8 %copy-start.1 = (bf16[2,3,320,640]{3,2,1,0:T(8,128)(2,1)S(1)}, bf16[2,3,320,640]{3,2,1,0:T(8,128)(2,1)}, u32[]{:S(2)}) copy-start(bf16[2,3,320,640]{3,2,1,0:T(8,128)(2,1)} %weights.9) | copy-start | bytes 7372804
  1.8 12.4 %copy-start.2 = (bf16[2,3,320,640]{3,2,1,0:T(8,128)(2,1)S(1)}, bf16[2,3,320,640]{3,2,1,0:T(8,128)(2,1)}, u32[]{:S(2)}) copy-start(bf16[2,3,320,640]{3,2,1,0:T(8,128)(2,1)} %weights.9) | copy-start | bytes 7372804
  3.0 39.1 %collective-permute-start.5 = (bf16[2,2,320,640]{3,2,1,0:T(8,128)(2,1)}, bf16[2,2,320,640]{3,2,1,0:T(8,128)(2,1)}, u32[]{:S(2)}, u32[]{:S(2)}) collective-permute-start(bf16[2,2,320,640]{3,2,1,0:T(8,128)(2,1)} %shard_map.91), channel_id=1, source_target_pairs={{0,4},{4,0},{8,12},{12,8},{16,20},{20,16},{24,28},{28,24},{1,5},{5... | collective-permute-start | bytes 4915208 | tf_op jit(solution)/shard_map/ppermute | solution.py:349
  6.1 1.1 copy-start.3
  7.2 0.9 copy-start.5
  8.2 0.9 copy-start.9
  9.7 9.0 %collective-permute-start = (bf16[6,24,640]{2,1,0:T(8,128)(2,1)S(1)}, bf16[6,24,640]{2,1,0:T(8,128)(2,1)S(1)}, u32[]{:S(2)}, u32[]{:S(2)}) collective-permute-start(bf16[6,24,640]{2,1,0:T(8,128)(2,1)S(1)} %get-tuple-element.42), channel_id=1, source_target_pairs={{0,8},{4,12},{8,0},{12,4},{16,24},{20,28},{24,16},{28,20},{1,9},{5... | collective-permute-start | bytes 552968 | tf_op jit(solution)/shard_map/ppermute | solution.py:352
  11.3 16.4 %collective-permute-start.1 = (bf16[6,24,640]{2,1,0:T(8,128)(2,1)S(1)}, bf16[6,24,640]{2,1,0:T(8,128)(2,1)S(1)}, u32[]{:S(2)}, u32[]{:S(2)}) collective-permute-start(bf16[6,24,640]{2,1,0:T(8,128)(2,1)S(1)} %get-tuple-element.43), channel_id=1, source_target_pairs={{0,16},{4,20},{8,24},{12,28},{16,0},{20,4},{24,8},{28,12},{1,17},{... | collective-permute-start | bytes 552968 | tf_op jit(solution)/shard_map/ppermute | solution.py:352
  13.9 13.8 %collective-permute-start.2 = (bf16[6,24,640]{2,1,0:T(8,128)(2,1)S(1)}, bf16[6,24,640]{2,1,0:T(8,128)(2,1)S(1)}, u32[]{:S(2)}, u32[]{:S(2)}) collective-permute-start(bf16[6,24,640]{2,1,0:T(8,128)(2,1)S(1)} %get-tuple-element.44), channel_id=1, source_target_pairs={{0,24},{4,28},{8,16},{12,20},{16,8},{20,12},{24,0},{28,4},{1,25},{... | collective-permute-start | bytes 552968 | tf_op jit(solution)/shard_map/ppermute | solution.py:352
  14.1 1.1 copy-start.4
  15.3 0.9 copy-start.6
  27.7 7.4 %collective-permute-start.6 = (bf16[2,96,640]{2,1,0:T(8,128)(2,1)S(1)}, bf16[2,96,640]{2,1,0:T(8,128)(2,1)S(1)}, u32[]{:S(2)}, u32[]{:S(2)}) collective-permute-start(bf16[2,96,640]{2,1,0:T(8,128)(2,1)S(1)} %get-tuple-element.49.refs_0_), channel_id=1, source_target_pairs={{0,8},{4,12},{8,0},{12,4},{16,24},{20,28},{24,16},{28,20},{1,9},{5... | collective-permute-start | bytes 737288 | tf_op jit(solution)/shard_map/ppermute | solution.py:352
  30.5 13.3 %collective-permute-start.3 = (bf16[4,2,24,640]{3,2,1,0:T(8,128)(2,1)S(1)}, bf16[4,2,24,640]{3,2,1,0:T(8,128)(2,1)S(1)}, u32[]{:S(2)}, u32[]{:S(2)}) collective-permute-start(bf16[4,2,24,640]{3,2,1,0:T(8,128)(2,1)S(1)} %shard_map.93.own), channel_id=1, source_target_pairs={{0,2},{1,3},{2,0},{3,1},{4,6},{5,7},{6,4},{7,5},{8,10},{9,11},{10,... | collective-permute-start | bytes 737288 | tf_op jit(solution)/shard_map/ppermute | solution.py:355
  42.1 10.7 %collective-permute-start.11 = (bf16[320,640]{1,0:T(8,128)(2,1)S(1)}, bf16[320,640]{1,0:T(8,128)(2,1)S(1)}, u32[]{:S(2)}, u32[]{:S(2)}) collective-permute-start(bf16[320,640]{1,0:T(8,128)(2,1)S(1)} %get-tuple-element.56), channel_id=1, source_target_pairs={{0,4},{4,0},{8,12},{12,8},{16,20},{20,16},{24,28},{28,24},{1,5},{5... | collective-permute-start | bytes 1228808 | tf_op jit(solution)/shard_map/ppermute | solution.py:349
  43.9 10.3 %collective-permute-start.4 = (bf16[2,4,2,24,640]{4,3,2,1,0:T(8,128)(2,1)S(1)}, bf16[2,4,2,24,640]{4,3,2,1,0:T(8,128)(2,1)S(1)}, u32[]{:S(2)}, u32[]{:S(2)}) collective-permute-start(bf16[2,4,2,24,640]{4,3,2,1,0:T(8,128)(2,1)S(1)} %shard_map.94.own), channel_id=1, source_target_pairs={{0,1},{1,0},{2,3},{3,2},{4,5},{5,4},{6,7},{7,6},{8,9},{9,8},{10,11... | collective-permute-start | bytes 1474568 | tf_op jit(solution)/shard_map/ppermute | solution.py:355
  44.0 20.3 %collective-permute-start.7 = (bf16[2,96,640]{2,1,0:T(8,128)(2,1)S(1)}, bf16[2,96,640]{2,1,0:T(8,128)(2,1)S(1)}, u32[]{:S(2)}, u32[]{:S(2)}) collective-permute-start(bf16[2,96,640]{2,1,0:T(8,128)(2,1)S(1)} %get-tuple-element.49.refs_0_), channel_id=1, source_target_pairs={{0,16},{4,20},{8,24},{12,28},{16,0},{20,4},{24,8},{28,12},{1,17},{... | collective-permute-start | bytes 737288 | tf_op jit(solution)/shard_map/ppermute | solution.py:352
  46.6 17.6 %collective-permute-start.8 = (bf16[2,96,640]{2,1,0:T(8,128)(2,1)S(1)}, bf16[2,96,640]{2,1,0:T(8,128)(2,1)S(1)}, u32[]{:S(2)}, u32[]{:S(2)}) collective-permute-start(bf16[2,96,640]{2,1,0:T(8,128)(2,1)S(1)} %get-tuple-element.49.refs_0_), channel_id=1, source_target_pairs={{0,24},{4,28},{8,16},{12,20},{16,8},{20,12},{24,0},{28,4},{1,25},{... | collective-permute-start | bytes 737288 | tf_op jit(solution)/shard_map/ppermute | solution.py:352
  52.8 31.6 %collective-permute-start.12 = (bf16[320,640]{1,0:T(8,128)(2,1)S(1)}, bf16[320,640]{1,0:T(8,128)(2,1)S(1)}, u32[]{:S(2)}, u32[]{:S(2)}) collective-permute-start(bf16[320,640]{1,0:T(8,128)(2,1)S(1)} %get-tuple-element.60), channel_id=1, source_target_pairs={{0,4},{4,0},{8,12},{12,8},{16,20},{20,16},{24,28},{28,24},{1,5},{5... | collective-permute-start | bytes 1228808 | tf_op jit(solution)/shard_map/ppermute | solution.py:349
  57.4 15.6 %collective-permute-start.10 = (bf16[1152,128]{1,0:T(8,128)(2,1)S(1)}, bf16[1152,128]{1,0:T(8,128)(2,1)S(1)}, u32[]{:S(2)}, u32[]{:S(2)}) collective-permute-start(bf16[1152,128]{1,0:T(8,128)(2,1)S(1)} %get-tuple-element.45), channel_id=1, source_target_pairs={{0,8},{4,12},{8,0},{12,4},{16,24},{20,28},{24,16},{28,20},{1,9},{5... | collective-permute-start | bytes 884744 | tf_op jit(solution)/shard_map/ppermute | solution.py:352
  67.4 17.0 %collective-permute-start.9 = (bf16[1152,128]{1,0:T(8,128)(2,1)S(1)}, bf16[1152,128]{1,0:T(8,128)(2,1)S(1)}, u32[]{:S(2)}, u32[]{:S(2)}) collective-permute-start(bf16[1152,128]{1,0:T(8,128)(2,1)S(1)} %get-tuple-element.52), channel_id=1, source_target_pairs={{0,8},{4,12},{8,0},{12,4},{16,24},{20,28},{24,16},{28,20},{1,9},{5... | collective-permute-start | bytes 884744 | tf_op jit(solution)/shard_map/ppermute | solution.py:352
  73.0 18.6 %collective-permute-start.17 = (bf16[768,128]{1,0:T(8,128)(2,1)S(1)}, bf16[768,128]{1,0:T(8,128)(2,1)S(1)}, u32[]{:S(2)}, u32[]{:S(2)}) collective-permute-start(bf16[768,128]{1,0:T(8,128)(2,1)S(1)} %get-tuple-element.69), channel_id=1, source_target_pairs={{0,16},{4,20},{8,24},{12,28},{16,0},{20,4},{24,8},{28,12},{1,17},{... | collective-permute-start | bytes 589832 | tf_op jit(solution)/shard_map/ppermute | solution.py:352
  84.5 14.9 %collective-permute-start.16 = (bf16[768,128]{1,0:T(8,128)(2,1)S(1)}, bf16[768,128]{1,0:T(8,128)(2,1)S(1)}, u32[]{:S(2)}, u32[]{:S(2)}) collective-permute-start(bf16[768,128]{1,0:T(8,128)(2,1)S(1)} %get-tuple-element.68), channel_id=1, source_target_pairs={{0,16},{4,20},{8,24},{12,28},{16,0},{20,4},{24,8},{28,12},{1,17},{... | collective-permute-start | bytes 589832 | tf_op jit(solution)/shard_map/ppermute | solution.py:352
  85.8 13.6 %copy-start.10 = (f32[640]{0:T(1024)S(1)}, f32[640]{0:T(1024)}, u32[]{:S(2)}) copy-start(f32[640]{0:T(1024)} %param.14) | copy-start | bytes 7684
  89.0 12.3 %copy-start.7 = (f32[480,128]{1,0:T(8,128)}, f32[480,128]{1,0:T(8,128)S(1)}, u32[]{:S(2)}) copy-start(f32[480,128]{1,0:T(8,128)S(1)} %get-tuple-element.64.total) | copy-start | bytes 737284
  89.0 24.6 %copy-start.11 = (f32[640]{0:T(1024)S(1)}, f32[640]{0:T(1024)}, u32[]{:S(2)}) copy-start(f32[640]{0:T(1024)} %param.13) | copy-start | bytes 7684
  89.0 7.9 %collective-permute-start.13 = (bf16[480,128]{1,0:T(8,128)(2,1)S(1)}, bf16[480,128]{1,0:T(8,128)(2,1)S(1)}, u32[]{:S(2)}, u32[]{:S(2)}) collective-permute-start(bf16[480,128]{1,0:T(8,128)(2,1)S(1)} %get-tuple-element.65), channel_id=1, source_target_pairs={{0,8},{4,12},{8,0},{12,4},{16,24},{20,28},{24,16},{28,20},{1,9},{5... | collective-permute-start | bytes 368648 | tf_op jit(solution)/shard_map/ppermute | solution.py:352
  91.6 9.7 %collective-permute-start.14 = (bf16[480,128]{1,0:T(8,128)(2,1)S(1)}, bf16[480,128]{1,0:T(8,128)(2,1)S(1)}, u32[]{:S(2)}, u32[]{:S(2)}) collective-permute-start(bf16[480,128]{1,0:T(8,128)(2,1)S(1)} %get-tuple-element.66), channel_id=1, source_target_pairs={{0,16},{4,20},{8,24},{12,28},{16,0},{20,4},{24,8},{28,12},{1,17},{... | collective-permute-start | bytes 368648 | tf_op jit(solution)/shard_map/ppermute | solution.py:352
  91.7 22.0 %collective-permute-start.19 = (bf16[768,128]{1,0:T(8,128)(2,1)S(1)}, bf16[768,128]{1,0:T(8,128)(2,1)S(1)}, u32[]{:S(2)}, u32[]{:S(2)}) collective-permute-start(bf16[768,128]{1,0:T(8,128)(2,1)S(1)} %shard_map.102.values_a), channel_id=1, source_target_pairs={{0,4},{4,0},{8,12},{12,8},{16,20},{20,16},{24,28},{28,24},{1,5},{5... | collective-permute-start | bytes 589832 | tf_op jit(solution)/shard_map/ppermute | solution.py:349
  100.2 13.5 %collective-permute-start.18 = (bf16[768,128]{1,0:T(8,128)(2,1)S(1)}, bf16[768,128]{1,0:T(8,128)(2,1)S(1)}, u32[]{:S(2)}, u32[]{:S(2)}) collective-permute-start(bf16[768,128]{1,0:T(8,128)(2,1)S(1)} %shard_map.103.keys_a), channel_id=1, source_target_pairs={{0,4},{4,0},{8,12},{12,8},{16,20},{20,16},{24,28},{28,24},{1,5},{5... | collective-permute-start | bytes 589832 | tf_op jit(solution)/shard_map/ppermute | solution.py:349
  101.3 11.3 %collective-permute-start.24 = (bf16[96,640]{1,0:T(8,128)(2,1)}, bf16[96,640]{1,0:T(8,128)(2,1)S(1)}, u32[]{:S(2)}, u32[]{:S(2)}) collective-permute-start(bf16[96,640]{1,0:T(8,128)(2,1)} %get-tuple-element.74.own), channel_id=1, source_target_pairs={{0,16},{4,20},{8,24},{12,28},{16,0},{20,4},{24,8},{28,12},{1,17},{... | collective-permute-start | bytes 368648 | tf_op jit(solution)/shard_map/ppermute | solution.py:352
  101.3 12.3 %collective-permute-start.15 = (bf16[480,128]{1,0:T(8,128)(2,1)}, bf16[480,128]{1,0:T(8,128)(2,1)S(1)}, u32[]{:S(2)}, u32[]{:S(2)}) collective-permute-start(bf16[480,128]{1,0:T(8,128)(2,1)} %get-tuple-element.67), channel_id=1, source_target_pairs={{0,24},{4,28},{8,16},{12,20},{16,8},{20,12},{24,0},{28,4},{1,25},{... | collective-permute-start | bytes 368648 | tf_op jit(solution)/shard_map/ppermute | solution.py:352
  103.5 27.0 %collective-permute-start.23 = (bf16[2,320,640]{2,1,0:T(8,128)(2,1)}, bf16[2,320,640]{2,1,0:T(8,128)(2,1)S(1)}, u32[]{:S(2)}, u32[]{:S(2)}) collective-permute-start(bf16[2,320,640]{2,1,0:T(8,128)(2,1)} %bitcast.58), channel_id=1, source_target_pairs={{0,4},{4,0},{8,12},{12,8},{16,20},{20,16},{24,28},{28,24},{1,5},{5... | collective-permute-start | bytes 2457608 | tf_op jit(solution)/shard_map/ppermute | solution.py:349
  113.5 10.3 %collective-permute-start.25 = (bf16[2,96,640]{2,1,0:T(8,128)(2,1)S(1)}, bf16[2,96,640]{2,1,0:T(8,128)(2,1)S(1)}, u32[]{:S(2)}, u32[]{:S(2)}) collective-permute-start(bf16[2,96,640]{2,1,0:T(8,128)(2,1)S(1)} %shard_map.105), channel_id=1, source_target_pairs={{0,8},{4,12},{8,0},{12,4},{16,24},{20,28},{24,16},{28,20},{1,9},{5... | collective-permute-start | bytes 737288 | tf_op jit(solution)/shard_map/ppermute | solution.py:352
  113.6 0.9 copy-start.8
  116.0 9.3 %collective-permute-start.20 = (bf16[480,128]{1,0:T(8,128)(2,1)S(1)}, bf16[480,128]{1,0:T(8,128)(2,1)S(1)}, u32[]{:S(2)}, u32[]{:S(2)}) collective-permute-start(bf16[480,128]{1,0:T(8,128)(2,1)S(1)} %shard_map.104), channel_id=1, source_target_pairs={{0,8},{4,12},{8,0},{12,4},{16,24},{20,28},{24,16},{28,20},{1,9},{5... | collective-permute-start | bytes 368648 | tf_op jit(solution)/shard_map/ppermute | solution.py:352
  118.1 12.1 %collective-permute-start.21 = (bf16[480,128]{1,0:T(8,128)(2,1)S(1)}, bf16[480,128]{1,0:T(8,128)(2,1)S(1)}, u32[]{:S(2)}, u32[]{:S(2)}) collective-permute-start(bf16[480,128]{1,0:T(8,128)(2,1)S(1)} %shard_map.104), channel_id=1, source_target_pairs={{0,16},{4,20},{8,24},{12,28},{16,0},{20,4},{24,8},{28,12},{1,17},{... | collective-permute-start | bytes 368648 | tf_op jit(solution)/shard_map/ppermute | solution.py:352
  118.1 12.2 %collective-permute-start.22 = (bf16[480,128]{1,0:T(8,128)(2,1)S(1)}, bf16[480,128]{1,0:T(8,128)(2,1)S(1)}, u32[]{:S(2)}, u32[]{:S(2)}) collective-permute-start(bf16[480,128]{1,0:T(8,128)(2,1)S(1)} %shard_map.104), channel_id=1, source_target_pairs={{0,24},{4,28},{8,16},{12,20},{16,8},{20,12},{24,0},{28,4},{1,25},{... | collective-permute-start | bytes 368648 | tf_op jit(solution)/shard_map/ppermute | solution.py:352
  125.0 5.6 %copy-start.12 = (bf16[2,640,320]{1,2,0:T(8,128)(2,1)S(1)}, bf16[2,640,320]{1,2,0:T(8,128)(2,1)}, u32[]{:S(2)}) copy-start(bf16[2,640,320]{1,2,0:T(8,128)(2,1)} %param.15) | copy-start | bytes 2457604
  132.7 1.9 %collective-permute-start.26 = (bf16[2,4,2,24,640]{4,3,0,1,2:T(8,128)(2,1)S(1)}, bf16[2,4,2,24,640]{4,3,0,1,2:T(8,128)(2,1)S(1)}, u32[]{:S(2)}, u32[]{:S(2)}) collective-permute-start(bf16[2,4,2,24,640]{4,3,0,1,2:T(8,128)(2,1)S(1)} %slice.154), channel_id=1, source_target_pairs={{0,1},{1,0},{2,3},{3,2},{4,5},{5,4},{6,7},{7,6},{8,9},{9,8},{10,11... | collective-permute-start | bytes 1474568 | tf_op jit(solution)/shard_map/ppermute | solution.py:355
  134.8 8.1 %collective-permute-start.27 = (bf16[2,4,24,640]{3,2,0,1:T(8,128)(2,1)S(1)}, bf16[2,4,24,640]{3,2,0,1:T(8,128)(2,1)S(1)}, u32[]{:S(2)}, u32[]{:S(2)}) collective-permute-start(bf16[2,4,24,640]{3,2,0,1:T(8,128)(2,1)S(1)} %fusion.15), channel_id=1, source_target_pairs={{0,2},{1,3},{2,0},{3,1},{4,6},{5,7},{6,4},{7,5},{8,10},{9,11},{10,... | collective-permute-start | bytes 737288 | tf_op jit(solution)/shard_map/ppermute | solution.py:355
  142.9 4.5 %collective-permute-start.28 = (bf16[2,24,640]{2,1,0:T(8,128)(2,1)S(1)}, bf16[2,24,640]{2,1,0:T(8,128)(2,1)S(1)}, u32[]{:S(2)}, u32[]{:S(2)}) collective-permute-start(bf16[2,24,640]{2,1,0:T(8,128)(2,1)S(1)} %get-tuple-element.84), channel_id=1, source_target_pairs={{0,8},{4,12},{8,0},{12,4},{16,24},{20,28},{24,16},{28,20},{1,9},{5... | collective-permute-start | bytes 184328 | tf_op jit(solution)/shard_map/ppermute | solution.py:352
  144.7 6.9 %collective-permute-start.29 = (bf16[2,24,640]{2,1,0:T(8,128)(2,1)S(1)}, bf16[2,24,640]{2,1,0:T(8,128)(2,1)S(1)}, u32[]{:S(2)}, u32[]{:S(2)}) collective-permute-start(bf16[2,24,640]{2,1,0:T(8,128)(2,1)S(1)} %get-tuple-element.83), channel_id=1, source_target_pairs={{0,16},{4,20},{8,24},{12,28},{16,0},{20,4},{24,8},{28,12},{1,17},{... | collective-permute-start | bytes 184328 | tf_op jit(solution)/shard_map/ppermute | solution.py:352
  144.9 6.8 %collective-permute-start.30 = (bf16[2,24,640]{2,1,0:T(8,128)(2,1)S(1)}, bf16[2,24,640]{2,1,0:T(8,128)(2,1)S(1)}, u32[]{:S(2)}, u32[]{:S(2)}) collective-permute-start(bf16[2,24,640]{2,1,0:T(8,128)(2,1)S(1)} %get-tuple-element.82), channel_id=1, source_target_pairs={{0,24},{4,28},{8,16},{12,20},{16,8},{20,12},{24,0},{28,4},{1,25},{... | collective-permute-start | bytes 184328 | tf_op jit(solution)/shard_map/ppermute | solution.py:352
where the time goes:
time: 153 us
  waiting for transfers between devices  76.3 us (50%)
  starting transfers between devices  46.8 us (31%)
  Pallas kernels  17.6 us (12%)
  local copies, waits for them, and re-layouts  8.32 us (5%)
  other arithmetic  1.97 us (1%)
    ppermute x21, waiting for transfers between devices, swap_z(): lax.ppermute(value, 'blk', [(i, i ^ 2 * step) for i in range(groups)])  56.2 us
    ppermute x21, starting transfers between devices, swap_z(): lax.ppermute(value, 'blk', [(i, i ^ 2 * step) for i in range(groups)])  35.6 us
    ppermute x6, waiting for transfers between devices, swap_x(): return lax.ppermute(value, 'blk', [(i, i ^ 1) for i in range(groups)])  11.8 us
    pallas_call x3, Pallas kernels, project(): call(functools.partial(project_kernel, part, size), outs, [VMEM] * len(ou...  9.39 us
    ppermute x4, waiting for transfers between devices, swap_u(): return lax.ppermute(value, 'uly', [(i, i ^ bit) for i in range(team)])  8.32 us
    unnamed x35, local copies, waits for them, and re-layouts  8 us
    ppermute x6, starting transfers between devices, swap_x(): return lax.ppermute(value, 'blk', [(i, i ^ 1) for i in range(groups)])  7.9 us
    ppermute x4, starting transfers between devices, swap_u(): return lax.ppermute(value, 'uly', [(i, i ^ bit) for i in range(team)])  3.33 us
  transfers between devices with their start and end apart: 31, of which 17 were waited for; matrix products, arithmetic and copies ran while one was open for 1% of the time, Pallas kernels for 10%

commit v1 on v0

--- a/solution.py
+++ b/solution.py
@@ -154,31 +154,37 @@
     return [(2 * part - 1).astype(jnp.float32) for part in parts]
 
 
-def prepare_kernel(team, place, tokens, in_bits, sign_bits, *blocks):
-    z = place[0]
+def sign_kernel(team, place, sign_bits, signs):
+    for part in range(signs.shape[0]):
+        pieces = sign_pieces(sign_bits.at[part], place[2], team)
+        signs[part] = jnp.concatenate(pieces, axis=0).astype(bf)
+
+
+def prepare_kernel(
+    team, place, tokens, in_bits, out_bits, mix_bits, weights, query_a, query_b, *refs
+):
+    blocks, sems = refs[:-1], refs[-1]
+    copies = [
+        pltpu.make_async_copy(weights.at[m, 0], out, sems.at[m])
+        for m, out in ((0, query_a), (1, query_b))
+    ]
+    for copy in copies:
+        copy.start()
+    z, u = place[0], place[2]
+    own_rows = tokens.shape[0]
     wide = tokens.shape[1] // len(blocks)
-    signs = [part.astype(bf) for part in sign_pieces(sign_bits.at[2], place[2], team)]
+    mix = [part.astype(bf) for part in sign_pieces(mix_bits, u, team)]
     for k, block in enumerate(blocks):
         cut = lanes(z ^ k, wide)
         plain = tokens[:, cut]
         sign = (2 * in_bits[:, cut] - 1).astype(jnp.float32)
         block[0] = plain
         block[1] = (plain.astype(jnp.float32) * sign).astype(bf)
+        for i, r in enumerate((0, 2)):
+            bits = out_bits[pl.ds(pl.multiple_of((u ^ r) * own_rows, 8), own_rows), cut]
+            block[2 + i] = (2 * bits - 1).astype(jnp.float32).astype(bf)
         for r in range(team):
-            block[2 + r] = signs[r]
-
-
-def rest_kernel(team, place, sign_bits, mix_bits, weights, query_a, query_b, signs, mix, sems):
-    copies = [
-        pltpu.make_async_copy(weights.at[m, 0], out, sems.at[m])
-        for m, out in ((0, query_a), (1, query_b))
-    ]
-    for copy in copies:
-        copy.start()
-    for part in (0, 1):
-        pieces = sign_pieces(sign_bits.at[part], place[2], team)
-        signs[part] = jnp.concatenate(pieces, axis=0).astype(bf)
-    mix[...] = jnp.concatenate(sign_pieces(mix_bits, place[2], team), axis=0).astype(bf)
+            block[4 + r] = mix[r]
     for copy in copies:
         copy.wait()
 
@@ -206,8 +212,10 @@
     out[...] = (total[...] + taken[...].astype(jnp.float32)).astype(bf)
 
 
-def project_kernel(part, size, place, rows, weights, partner_0, partner_1, *refs):
-    held, total, sems = refs[-3:]
+def project_kernel(
+    part, size, place, rows, weights, partner_0, partner_1, all_signs,
+    send, keep_own, keep_two, held, total, signs, sems, sign_sems,
+):
     z, x = place[0], place[1]
     slab = weights.shape[2]
     partner = (partner_0, partner_1)
@@ -215,30 +223,26 @@
         partner = (partner_0.at[0, part - 1], partner_0.at[1, part - 1])
     own = pl.ds(pl.multiple_of(x * slab, 64), slab)
     other = pl.ds(pl.multiple_of((1 - x) * slab, 64), slab)
+    depth = rows.shape[1] // size
     copies = []
     for m in (0, 1):
         copies.append(
             pltpu.make_async_copy(weights.at[m, part], held.at[m, own], sems.at[m, 0])
         )
         copies.append(pltpu.make_async_copy(partner[m], held.at[m, other], sems.at[m, 1]))
+    for j in range(depth):
+        copies.append(
+            pltpu.make_async_copy(all_signs.at[z ^ j, part], signs.at[j], sign_sems.at[j])
+        )
     for copy in copies:
         copy.start()
     for copy in copies:
         copy.wait()
-    depth = rows.shape[1] // size
-    outs = refs[depth:-3]
-
-    def sign(j):
-        if part < 2:
-            return refs[j][part].astype(jnp.float32)
-        pieces = [refs[j][r] for r in range(2, refs[j].shape[0])]
-        return jnp.concatenate([piece.astype(jnp.float32) for piece in pieces], axis=0)
-
     total[...] = dot32(rows[1], held[1])
     plain = dot32(rows[0], held[0])
     for j in range(depth):
         cut = slice(j * size, (j + 1) * size)
-        total[cut] = plain[cut] + sign(j) * total[cut]
+        total[cut] = plain[cut] + signs[j].astype(jnp.float32) * total[cut]
 
     def block(j, head):
         return total[j * size : (j + 1) * size, lanes(head, HEAD)]
@@ -252,23 +256,28 @@
         target[start : start + size] = block(j, depth).astype(target.dtype)
 
     half = depth * size
+    main(keep_own, 0, 0)
+    main(keep_two, 0, 2)
+    main(send, 0, 1)
     if part:
-        send, keep_own, keep_two = outs
-        main(send, 0, 1)
         main(send, half, 3)
         for j in range(depth):
             rest(send, 2 * half + (j ^ 1) * size, j)
             rest(keep_own, half + j * size, j)
-        main(keep_own, 0, 0)
-        main(keep_two, 0, 2)
     else:
-        for k in range(depth):
-            main(outs[k], 0, k)
-            rest(outs[k], half, k)
+        rest(send, half, 1)
+        main(send, half + size, 3)
+        rest(send, 2 * half + size, 3)
+        rest(keep_own, half, 0)
+        rest(keep_two, half, 2)
 
 
 def middle_kernel(size, keep_own, keep_two, taken, send, total):
     half = keep_two.shape[0]
+    if keep_own.shape[0] == half:
+        total[...] = keep_own[...] + taken[:half].astype(jnp.float32)
+        send[...] = (keep_two[...] + taken[half:].astype(jnp.float32)).astype(bf)
+        return
     total[:half] = keep_own[:half] + taken[:half].astype(jnp.float32)
     send[:half] = (keep_two[...] + taken[half : 2 * half].astype(jnp.float32)).astype(bf)
     for j in range(half // size):
@@ -294,12 +303,9 @@
 
 
 def attend_kernel(
-    half, place, total, taken_1, taken_2, taken_3, gain, keys_a, keys_b, values_a, values_b, out
+    half, place, total, taken, gain, keys_a, keys_b, values_a, values_b, out
 ):
-    keep = total[...]
-    for taken in (taken_1, taken_2, taken_3):
-        keep = keep + taken[...].astype(jnp.float32)
-    keep = keep.astype(bf)
+    keep = (total[...] + taken[...].astype(jnp.float32)).astype(bf)
     heads = gain.shape[0]
 
     def attend(queries, cut):
@@ -318,12 +324,10 @@
     out[half:] = attend(last, slice(half, 2 * half))
 
 
-def final_kernel(place, bits, *refs):
+def final_kernel(place, *refs):
     out = refs[-1]
     for k, block in enumerate(refs[:-1]):
-        cut = lanes(place[0] ^ k, block.shape[2])
-        sign = (2 * bits[:, cut] - 1).astype(jnp.float32)
-        out[:, cut] = (block[0].astype(jnp.float32) + sign * block[1].astype(jnp.float32)).astype(bf)
+        out[:, lanes(place[0] ^ k, block.shape[1])] = block[...]
 
 
 def stationary_plan(
@@ -364,93 +368,85 @@
     partner_early = swap_x(early)
 
     sign_bits = jnp.transpose(qkv_bits, (1, 0, 2))
-    blocks = call(
+    sign_own = call(
+        functools.partial(sign_kernel, team), shape(3, size, columns), VMEM, [SMEM, VMEM]
+    )(place, sign_bits)
+    all_signs = lax.all_gather(
+        sign_own, "blk", axis=0, axis_index_groups=[[2 * i + j for i in steps] for j in (0, 1)]
+    )
+
+    query_a, query_b, *blocks = call(
         functools.partial(prepare_kernel, team),
-        [shape(2 + team, own_rows, 2 * slab)] * depth, [VMEM] * depth, [SMEM] + [VMEM] * 3,
-    )(place, after(tokens, early), in_bits, sign_bits)
+        [shape(slab, columns)] * 2 + [shape(4 + team, own_rows, 2 * slab)] * depth,
+        [ANY] * 2 + [VMEM] * depth,
+        [SMEM] + [VMEM] * 4 + [ANY],
+        [pltpu.SemaphoreType.DMA((2,))],
+    )(place, after(tokens, early, sign_own), in_bits, out_bits, mix_bits, qkv_weights)
     got = [blocks[0]] + [swap_z(blocks[k], k) for k in steps if k]
-    query_a, query_b, sign_pair, mix_own = call(
-        functools.partial(rest_kernel, team),
-        [shape(slab, columns), shape(slab, columns), shape(2, size, columns), shape(size, columns)],
-        [ANY, ANY, VMEM, VMEM],
-        [SMEM, VMEM, VMEM, ANY],
-        [pltpu.SemaphoreType.DMA((2,))],
-    )(place, after(sign_bits, blocks[0]), mix_bits, qkv_weights)
-    sent_pair = after(sign_pair, *got[1:])
-    pairs = [sign_pair] + [swap_z(sent_pair, k) for k in steps if k]
-    signs = {2: got, 1: pairs, 0: pairs}
-
     held_shape = (depth, 2, own_rows, 2 * slab)
     held = call(stack_kernel, shape(*held_shape), VMEM, [VMEM] * depth)(*got)
     held = call(pair_kernel, shape(2, *held_shape), VMEM, [VMEM] * 2)(held, swap_u(held, 2))
     rows = call(rows_kernel, shape(2, half, 2 * slab), VMEM, [VMEM] * 2)(held, swap_u(held, 1))
 
-    query_a = swap_x(after(query_a, partner_early, pairs[1]))
+    query_a = swap_x(after(query_a, partner_early, rows))
     query_b = swap_x(after(query_b, query_a))
     partner = {2: [partner_early] * 2, 1: [partner_early] * 2, 0: [query_a, query_b]}
 
-    def project(part, rows, outs):
+    def project(part, rows):
+        counts = (3 * half, 2 * half, half) if part else (2 * (half + size),) + (half + size,) * 2
         return call(
             functools.partial(project_kernel, part, size),
-            outs,
-            [VMEM] * len(outs),
-            [SMEM, VMEM, ANY, ANY, ANY] + [VMEM] * len(signs[part]),
+            [shape(counts[0], HEAD)] + [shape(count, HEAD, dtype=f32) for count in counts[1:]],
+            [VMEM] * 3,
+            [SMEM, VMEM] + [ANY] * 4,
             [
                 pltpu.VMEM((2, 2 * slab, columns), bf),
                 pltpu.VMEM((half, columns), f32),
+                pltpu.VMEM((depth, size, columns), bf),
                 pltpu.SemaphoreType.DMA((2, 2)),
+                pltpu.SemaphoreType.DMA((depth,)),
             ],
-        )(place, rows, qkv_weights, *partner[part], *signs[part])
-
-    two_step = [
-        shape(3 * half, HEAD), shape(2 * half, HEAD, dtype=f32), shape(half, HEAD, dtype=f32)
-    ]
+        )(place, rows, qkv_weights, *partner[part], all_signs)
 
     def middle(keep_own, keep_two, taken):
+        count = keep_own.shape[0]
         return call(
             functools.partial(middle_kernel, size),
-            [shape(2 * half, HEAD), shape(2 * half, HEAD, dtype=f32)],
+            [shape(count, HEAD), shape(count, HEAD, dtype=f32)],
             [VMEM] * 2,
             [VMEM] * 3,
         )(keep_own, keep_two, taken)
 
-    value_send, keep_own, keep_two = project(2, rows, two_step)
-    key_send, key_own, key_two = project(1, after(rows, value_send), two_step)
+    value_send, keep_own, keep_two = project(2, rows)
+    key_send, key_own, key_two = project(1, after(rows, value_send))
     taken = after(swap_z(value_send, 1), key_send, query_a)
     send, value_total = middle(keep_own, keep_two, taken)
     value_last = swap_z(send, 2)
-    taken = after(swap_z(key_send, 1), value_total, query_b)
+    taken = after(swap_z(key_send, 1), value_last, query_b)
     send, key_total = middle(key_own, key_two, taken)
     key_last = swap_z(send, 2)
-    own, *sends = project(
-        0,
-        after(rows, key_total),
-        [shape(half + size, HEAD, dtype=f32)] + [shape(half + size, HEAD)] * 3,
-    )
-    taken_q = [swap_z(sends[k - 1], k) for k in steps if k]
+    query_send, query_own, query_two = project(0, after(rows, key_total))
+    taken = swap_z(query_send, 1)
     values = call(sum_kernel, shape(2 * half, HEAD), VMEM, [VMEM] * 2)(
-        value_total, after(value_last, own)
+        value_total, after(value_last, query_send)
     )
     values_partner = swap_x(values)
     keys = call(
         functools.partial(key_kernel, half), shape(2 * half, HEAD), VMEM, [SMEM] + [VMEM] * 3
-    )(place, key_total, after(key_last, values, taken_q[0]), gain_key.reshape(heads, HEAD))
+    )(place, key_total, after(key_last, values), gain_key.reshape(heads, HEAD))
     keys_partner = swap_x(keys)
-    mix_two = swap_z(after(mix_own, taken_q[1]), 2)
-    mix_13 = swap_z(
-        call(pair_kernel, shape(2, size, columns), VMEM, [VMEM] * 2)(mix_own, mix_two), 1
-    )
+    send, query_total = middle(query_own, query_two, taken)
     out_t = jnp.transpose(out_weights, (0, 2, 1))
-    out_partner = swap_x(after(out_t, keys, taken_q[1]))
+    out_partner = swap_x(after(out_t, keys, query_total))
 
     done = call(
         functools.partial(attend_kernel, half),
         shape(half + size, HEAD),
         VMEM,
-        [SMEM] + [VMEM] * 9,
+        [SMEM] + [VMEM] * 7,
     )(
-        place, own, *taken_q,
-        gain_query.reshape(heads, HEAD), keys, keys_partner, values, values_partner,
+        place, query_total, swap_z(send, 2), gain_query.reshape(heads, HEAD),
+        keys, keys_partner, values, values_partner,
     )
 
     by_head, last_head = [], []
@@ -467,7 +463,7 @@
         ] + [lax.slice_in_dim(value, depth * HEAD, heads * HEAD, axis=axis)]
         return jnp.concatenate(parts, axis=axis)
 
-    mix = relative(jnp.concatenate([mix_own, mix_13[0], mix_two, mix_13[1]], axis=0), 1)
+    mix = relative(jnp.concatenate([g[4:].reshape(size, columns) for g in got], axis=0), 1)
     attended_flipped = attended * mix
     first = jnp.where(x == 0, out_t, out_partner)
     second = jnp.where(x == 0, out_partner, out_t)
@@ -477,12 +473,13 @@
     ).astype(bf)
     partial = partial.reshape(2, depth, team, own_rows, 2 * slab)
     summed = partial[:, :, 0::2].astype(f32) + swap_u(partial[:, :, 1::2], 1).astype(f32)
-    summed = (summed[:, :, 0] + swap_u(summed[:, :, 1].astype(bf), 2).astype(f32)).astype(bf)
-    final = [summed[:, 0]] + [swap_z(summed[:, k], k) for k in steps if k]
-    own_bits = lax.dynamic_slice_in_dim(out_bits, u * own_rows, own_rows, 0)
+    out_signs = jnp.stack([g[2:4] for g in got]).astype(f32)
+    summed = summed[0] + out_signs * summed[1]
+    summed = (summed[:, 0] + swap_u(summed[:, 1].astype(bf), 2).astype(f32)).astype(bf)
+    final = [summed[0]] + [swap_z(summed[k], k) for k in steps if k]
     return call(
-        final_kernel, shape(own_rows, width), VMEM, [SMEM] + [VMEM] * (1 + depth)
-    )(place, own_bits, *final)
+        final_kernel, shape(own_rows, width), VMEM, [SMEM] + [VMEM] * depth
+    )(place, *final)
 
 
 def body(*arrays):

time: 153 us -> 171 us (1.12)
  between operations: 0.48 us -> 14 us
  local copies, waits for them, and re-layouts: 8.32 us -> 17.7 us
  waiting for transfers between devices: 76.3 us -> 68.8 us
  Pallas kernels: 17.6 us -> 19.6 us
    ppermute x21 -> x15, waiting for transfers between devices: 56.2 us -> 48.1 us  [swap_z(): lax.ppermute(value, 'blk', [(i, i ^ 2 * step) for i in range(groups)])]
    ppermute x6, waiting for transfers between devices: 11.8 us -> 4.7 us  [swap_x(): return lax.ppermute(value, 'blk', [(i, i ^ 1) for i in range(groups)])]
    all_gather x0 -> x1, waiting for transfers between devices: none -> 5.37 us  [stationary_plan(): lax.all_gather(sign_own, 'blk', axis=0, axis_index_groups=[[2 * i + j for...]
    slice x0 -> x4, local copies, waits for them, and re-layouts: none -> 4.42 us  [stationary_plan(): g[4:].reshape(size, columns)]
    another operation x0 -> x4, local copies, waits for them, and re-layouts: none -> 3.34 us  [stationary_plan(): out_signs = jnp.stack([g[2:4] for g in got]).astype(f32)]
    ppermute x4, waiting for transfers between devices: 8.32 us -> 10.6 us  [swap_u(): return lax.ppermute(value, 'uly', [(i, i ^ bit) for i in range(team)])]
    pallas_call x9, Pallas kernels: 14 us -> 16.1 us  [the longest x3 10.2 us: project(): call(functools.partial(project_kernel, part, size), [shape(counts[0], HEA...]
    unnamed x35 -> x57, local copies, waits for them, and re-layouts: 8 us -> 9.66 us
  transfers between devices with their start and end apart: 31 -> 26, of which waited for: 17 -> 16; matrix products, arithmetic and copies ran while one was open for 1% -> 5% of each run, Pallas kernels for 10% -> 8%
where the time goes in v1:
time: 171 us; the launch traced here: 170 us
  waiting for transfers between devices  68.8 us (40%)
  starting transfers between devices  46.5 us (27%)
  Pallas kernels  19.6 us (11%)
  local copies, waits for them, and re-layouts  17.7 us (10%)
  between operations  14 us (8%)
  other arithmetic  2.03 us (1%)
    ppermute x15, waiting for transfers between devices, swap_z(): lax.ppermute(value, 'blk', [(i, i ^ 2 * step) for i in range(groups)])  48.1 us
    ppermute x15, starting transfers between devices, swap_z(): lax.ppermute(value, 'blk', [(i, i ^ 2 * step) for i in range(groups)])  35.6 us
    ppermute x4, waiting for transfers between devices, swap_u(): return lax.ppermute(value, 'uly', [(i, i ^ bit) for i in range(team)])  10.6 us
    pallas_call x3, Pallas kernels, project(): call(functools.partial(project_kernel, part, size), [shape(counts[0], HEA...  10.2 us
    unnamed x57, local copies, waits for them, and re-layouts  9.66 us
    ppermute x6, starting transfers between devices, swap_x(): return lax.ppermute(value, 'blk', [(i, i ^ 1) for i in range(groups)])  7.51 us
    all_gather x1, waiting for transfers between devices, stationary_plan(): lax.all_gather(sign_own, 'blk', axis=0, axis_index_groups=[[2 * i + j for...  5.37 us
    ppermute x6, waiting for transfers between devices, swap_x(): return lax.ppermute(value, 'blk', [(i, i ^ 1) for i in range(groups)])  4.7 us
  transfers between devices with their start and end apart: 26, of which 16 were waited for; matrix products, arithmetic and copies ran while one was open for 5% of the time, Pallas kernels for 8%

profile of v1, /device:TPU:0, one launch (start us, length us, event | category | flops | bytes accessed | tf_op | source)
XLA Modules:
  0.0 170.0 jit_solution(11481281755066811585)
XLA Ops:
  6.6 1.1 copy-done.11
  7.7 1.4 shard_map.92
  9.2 1.7 copy-done
  11.1 3.0 %collective-permute-start.5 = (bf16[2,2,320,640]{3,2,1,0:T(8,128)(2,1)S(1)}, bf16[2,2,320,640]{3,2,1,0:T(8,128)(2,1)S(1)}, u32[]{:S(2)}, u32[]{:S(2)}) collective-permute-start(bf16[2,2,320,640]{3,2,1,0:T(8,128)(2,1)S(1)} %shard_map.91), channel_id=1, source_target_pairs={{0,4},{4,0},{8,12},{12,8},{16,20},{20,16},{24,28},{28,24},{1,5},{5... | collective-permute-start | bytes 4915208 | tf_op jit(solution)/shard_map/ppermute | solution.py:353
  14.1 1.5 shard_map.93
  15.6 1.9 %collective-permute-start = (bf16[8,24,640]{2,1,0:T(8,128)(2,1)S(1)}, bf16[8,24,640]{2,1,0:T(8,128)(2,1)S(1)}, u32[]{:S(2)}, u32[]{:S(2)}) collective-permute-start(bf16[8,24,640]{2,1,0:T(8,128)(2,1)S(1)} %get-tuple-element.38), channel_id=1, source_target_pairs={{0,8},{4,12},{8,0},{12,4},{16,24},{20,28},{24,16},{28,20},{1,9},{5... | collective-permute-start | bytes 737288 | tf_op jit(solution)/shard_map/ppermute | solution.py:356
  17.5 2.6 %collective-permute-start.1 = (bf16[8,24,640]{2,1,0:T(8,128)(2,1)S(1)}, bf16[8,24,640]{2,1,0:T(8,128)(2,1)S(1)}, u32[]{:S(2)}, u32[]{:S(2)}) collective-permute-start(bf16[8,24,640]{2,1,0:T(8,128)(2,1)S(1)} %get-tuple-element.39), channel_id=1, source_target_pairs={{0,16},{4,20},{8,24},{12,28},{16,0},{20,4},{24,8},{28,12},{1,17},{... | collective-permute-start | bytes 737288 | tf_op jit(solution)/shard_map/ppermute | solution.py:356
  20.1 13.5 %collective-permute-done.refs_1_ = bf16[8,24,640]{2,1,0:T(8,128)(2,1)S(1)} collective-permute-done((bf16[8,24,640]{2,1,0:T(8,128)(2,1)S(1)}, bf16[8,24,640]{2,1,0:T(8,128)(2,1)S(1)}, u32[]{:S(2)}, u32[]{:S(2)}) %collective-permute-start) | collective-permute-done | bytes 245792 | tf_op jit(solution)/shard_map/ppermute | solution.py:356
  33.6 13.0 %collective-permute-done.1.refs_2_ = bf16[8,24,640]{2,1,0:T(8,128)(2,1)S(1)} collective-permute-done((bf16[8,24,640]{2,1,0:T(8,128)(2,1)S(1)}, bf16[8,24,640]{2,1,0:T(8,128)(2,1)S(1)}, u32[]{:S(2)}, u32[]{:S(2)}) %collective-permute-start.1) | collective-permute-done | bytes 245792 | tf_op jit(solution)/shard_map/ppermute | solution.py:356
  46.6 2.6 %collective-permute-done.2.refs_3_ = bf16[8,24,640]{2,1,0:T(8,128)(2,1)S(1)} collective-permute-done((bf16[8,24,640]{2,1,0:T(8,128)(2,1)S(1)}, bf16[8,24,640]{2,1,0:T(8,128)(2,1)S(1)}, u32[]{:S(2)}, u32[]{:S(2)}) %collective-permute-start.2) | collective-permute-done | bytes 245792 | tf_op jit(solution)/shard_map/ppermute | solution.py:356
  49.2 1.6 collective-permute-start.3
  50.9 4.6 %collective-permute-done.3.taken = bf16[4,2,24,640]{3,2,1,0:T(8,128)(2,1)S(1)} collective-permute-done((bf16[4,2,24,640]{3,2,1,0:T(8,128)(2,1)S(1)}, bf16[4,2,24,640]{3,2,1,0:T(8,128)(2,1)S(1)}, u32[]{:S(2)}, u32[]{:S(2)}) %collective-permute-start.3) | collective-permute-done | bytes 245792 | tf_op jit(solution)/shard_map/ppermute | solution.py:359
  55.6 1.9 %collective-permute-done.4.taken = bf16[2,4,2,24,640]{4,3,2,1,0:T(8,128)(2,1)S(1)} collective-permute-done((bf16[2,4,2,24,640]{4,3,2,1,0:T(8,128)(2,1)S(1)}, bf16[2,4,2,24,640]{4,3,2,1,0:T(8,128)(2,1)S(1)}, u32[]{:S(2)}, u32[]{:S(2)}) %collective-permute-start.4) | collective-permute-done | bytes 491552 | tf_op jit(solution)/shard_map/ppermute | solution.py:359
  57.6 1.2 copy-done.2
  58.8 1.5 collective-permute-start.8
  60.4 5.4 %all-gather.3.cloned.1.call-done = bf16[12,96,640]{2,1,0:T(8,128)(2,1)} async-done(((bf16[3,96,640]{2,1,0:T(8,128)(2,1)}), bf16[12,96,640]{2,1,0:T(8,128)(2,1)}) %all-gather.3.cloned.1.call-update) | async-done | bytes 1474576 | tf_op jit(solution)/shard_map/all_gather | solution.py:374
  65.7 1.4 copy-done.3
  67.2 1.4 copy-done.4
  68.5 3.2 %shard_map.97 = (bf16[1152,128]{1,0:T(8,128)(2,1)S(1)}, f32[768,128]{1,0:T(8,128)S(1)}, f32[384,128]{1,0:T(8,128)S(1)}) custom-call(s32[3]{0:T(128)S(1)} %pad_add_fusion.place, bf16[2,384,640]{2,1,0:T(8,128)(2,1)S(1)} %shard_map.96.rows, bf16[2,3,320,640]{3,2,1,0:T(8,128)(2,1)S(1)} %copy-done.1, bf16[2,2,320,640]{3,2,1,0:T(8,128)(2,1)S(1)} %copy-done.3, ...), custom_call_target="tpu_custom_call" | custom-call | tf_op jit(solution)/shard_map/pallas_call | solution.py:397
  71.7 8.8 %collective-permute-start.7 = (bf16[1152,128]{1,0:T(8,128)(2,1)S(1)}, bf16[1152,128]{1,0:T(8,128)(2,1)S(1)}, u32[]{:S(2)}, u32[]{:S(2)}) collective-permute-start(bf16[1152,128]{1,0:T(8,128)(2,1)S(1)} %get-tuple-element.41), channel_id=1, source_target_pairs={{0,8},{4,12},{8,0},{12,4},{16,24},{20,28},{24,16},{28,20},{1,9},{5... | collective-permute-start | bytes 884744 | tf_op jit(solution)/shard_map/ppermute | solution.py:356
  81.2 3.9 %shard_map.98 = (bf16[1152,128]{1,0:T(8,128)(2,1)}, f32[768,128]{1,0:T(8,128)S(1)}, f32[384,128]{1,0:T(8,128)S(1)}) custom-call(s32[3]{0:T(128)S(1)} %pad_add_fusion.place, bf16[2,384,640]{2,1,0:T(8,128)(2,1)S(1)} %shard_map.96.rows, bf16[2,3,320,640]{3,2,1,0:T(8,128)(2,1)S(1)} %copy-done.1, bf16[2,2,320,640]{3,2,1,0:T(8,128)(2,1)S(1)} %copy-done.3, ...), custom_call_target="tpu_custom_call" | custom-call | tf_op jit(solution)/shard_map/pallas_call | solution.py:397
  85.9 5.1 %collective-permute-start.6 = (bf16[1152,128]{1,0:T(8,128)(2,1)}, bf16[1152,128]{1,0:T(8,128)(2,1)}, u32[]{:S(2)}, u32[]{:S(2)}) collective-permute-start(bf16[1152,128]{1,0:T(8,128)(2,1)} %get-tuple-element.45), channel_id=1, source_target_pairs={{0,8},{4,12},{8,0},{12,4},{16,24},{20,28},{24,16},{28,20},{1,9},{5... | collective-permute-start | bytes 884744 | tf_op jit(solution)/shard_map/ppermute | solution.py:356
  92.5 1.9 %collective-permute-start.9 = (bf16[768,128]{1,0:T(8,128)(2,1)}, bf16[768,128]{1,0:T(8,128)(2,1)}, u32[]{:S(2)}, u32[]{:S(2)}) collective-permute-start(bf16[768,128]{1,0:T(8,128)(2,1)} %get-tuple-element.51), channel_id=1, source_target_pairs={{0,16},{4,20},{8,24},{12,28},{16,0},{20,4},{24,8},{28,12},{1,17},{... | collective-permute-start | bytes 589832 | tf_op jit(solution)/shard_map/ppermute | solution.py:356
  95.3 1.6 slice.173
  96.8 1.0 slice.209
  97.9 0.9 slice.210
  99.7 0.9 pad_maximum_fusion.1
  100.7 1.1 collective-permute-done.6.taken
  101.7 1.0 copy-done.13
  102.7 1.0 shard_map.100
  103.8 3.2 %shard_map.101 = (bf16[960,128]{1,0:T(8,128)(2,1)S(1)}, f32[480,128]{1,0:T(8,128)S(1)}, f32[480,128]{1,0:T(8,128)S(1)}) custom-call(s32[3]{0:T(128)S(1)} %pad_add_fusion.place, bf16[2,384,640]{2,1,0:T(8,128)(2,1)S(1)} %shard_map.96.rows, bf16[2,3,320,640]{3,2,1,0:T(8,128)(2,1)S(1)} %copy-done.1, bf16[320,640]{1,0:T(8,128)(2,1)} %collective-permute-done.8.partner_0, ...), custom_call_target="tpu_custom_call" | custom-call | tf_op jit(solution)/shard_map/pallas_call | solution.py:397
  106.9 3.7 %collective-permute-start.11 = (bf16[960,128]{1,0:T(8,128)(2,1)S(1)}, bf16[960,128]{1,0:T(8,128)(2,1)S(1)}, u32[]{:S(2)}, u32[]{:S(2)}) collective-permute-start(bf16[960,128]{1,0:T(8,128)(2,1)S(1)} %get-tuple-element.59), channel_id=1, source_target_pairs={{0,8},{4,12},{8,0},{12,4},{16,24},{20,28},{24,16},{28,20},{1,9},{5... | collective-permute-start | bytes 737288 | tf_op jit(solution)/shard_map/ppermute | solution.py:356
  110.8 2.1 %collective-permute-start.13 = (bf16[768,128]{1,0:T(8,128)(2,1)S(1)}, bf16[768,128]{1,0:T(8,128)(2,1)S(1)}, u32[]{:S(2)}, u32[]{:S(2)}) collective-permute-start(bf16[768,128]{1,0:T(8,128)(2,1)S(1)} %get-tuple-element.62), channel_id=1, source_target_pairs={{0,16},{4,20},{8,24},{12,28},{16,0},{20,4},{24,8},{28,12},{1,17},{... | collective-permute-start | bytes 589832 | tf_op jit(solution)/shard_map/ppermute | solution.py:356
  112.9 1.0 shard_map.103.values_a
  114.6 7.4 %collective-permute-done.13.taken = bf16[768,128]{1,0:T(8,128)(2,1)S(1)} collective-permute-done((bf16[768,128]{1,0:T(8,128)(2,1)S(1)}, bf16[768,128]{1,0:T(8,128)(2,1)S(1)}, u32[]{:S(2)}, u32[]{:S(2)}) %collective-permute-start.13) | collective-permute-done | bytes 196640 | tf_op jit(solution)/shard_map/ppermute | solution.py:356
  123.5 1.6 collective-permute-start.19
  125.1 4.1 %collective-permute-done.12.taken = bf16[480,128]{1,0:T(8,128)(2,1)S(1)} collective-permute-done((bf16[480,128]{1,0:T(8,128)(2,1)S(1)}, bf16[480,128]{1,0:T(8,128)(2,1)S(1)}, u32[]{:S(2)}, u32[]{:S(2)}) %collective-permute-start.12) | collective-permute-done | bytes 122912 | tf_op jit(solution)/shard_map/ppermute | solution.py:356
  129.2 1.4 collective-permute-done.14.keys_b
  130.6 1.4 shard_map.105
  132.2 4.3 %collective-permute-start.16 = (bf16[480,128]{1,0:T(8,128)(2,1)S(1)}, bf16[480,128]{1,0:T(8,128)(2,1)S(1)}, u32[]{:S(2)}, u32[]{:S(2)}) collective-permute-start(bf16[480,128]{1,0:T(8,128)(2,1)S(1)} %shard_map.105), channel_id=1, source_target_pairs={{0,8},{4,12},{8,0},{12,4},{16,24},{20,28},{24,16},{28,20},{1,9},{5... | collective-permute-start | bytes 368648 | tf_op jit(solution)/shard_map/ppermute | solution.py:356
  136.6 3.7 %collective-permute-done.16 = bf16[480,128]{1,0:T(8,128)(2,1)S(1)} collective-permute-done((bf16[480,128]{1,0:T(8,128)(2,1)S(1)}, bf16[480,128]{1,0:T(8,128)(2,1)S(1)}, u32[]{:S(2)}, u32[]{:S(2)}) %collective-permute-start.16) | collective-permute-done | bytes 122912 | tf_op jit(solution)/shard_map/ppermute | solution.py:356
  141.5 3.3 %collective-permute-done.19 = bf16[2,320,640]{2,1,0:T(8,128)(2,1)S(1)} collective-permute-done((bf16[2,320,640]{2,1,0:T(8,128)(2,1)S(1)}, bf16[2,320,640]{2,1,0:T(8,128)(2,1)S(1)}, u32[]{:S(2)}, u32[]{:S(2)}) %collective-permute-start.19) | collective-permute-done | bytes 819232 | tf_op jit(solution)/shard_map/ppermute | solution.py:353
  149.7 1.6 collective-permute-start.21
  151.4 4.2 %collective-permute-done.21 = bf16[4,24,640]{2,1,0:T(8,128)(2,1)S(1)} collective-permute-done((bf16[4,24,640]{2,1,0:T(8,128)(2,1)S(1)}, bf16[4,24,640]{2,1,0:T(8,128)(2,1)S(1)}, u32[]{:S(2)}, u32[]{:S(2)}) %collective-permute-start.21) | collective-permute-done | bytes 122912 | tf_op jit(solution)/shard_map/ppermute | solution.py:359
  155.7 1.1 collective-permute-start.23
  156.8 3.2 %collective-permute-start.22 = (bf16[24,640]{1,0:T(8,128)(2,1)S(1)}, bf16[24,640]{1,0:T(8,128)(2,1)S(1)}, u32[]{:S(2)}, u32[]{:S(2)}) collective-permute-start(bf16[24,640]{1,0:T(8,128)(2,1)S(1)} %get-tuple-element.76), channel_id=1, source_target_pairs={{0,8},{4,12},{8,0},{12,4},{16,24},{20,28},{24,16},{28,20},{1,9},{5... | collective-permute-start | bytes 92168 | tf_op jit(solution)/shard_map/ppermute | solution.py:356
  160.0 1.3 collective-permute-done.24.refs_3_
  161.9 1.2 shard_map.106
  (114 shorter events, 14.4 us)
Async XLA Ops:
  6.5 59.2 %all-gather.3.cloned.1.call-start = ((), (), s32[]{:S(2)}) async-start(), calls=%async_computation | async-start | bytes 1843200 | tf_op jit(solution)/shard_map/all_gather | solution.py:374
  6.6 1.1 copy-start.11
  9.2 1.7 copy-start
  10.8 3.3 %copy-start.1 = (bf16[2,3,320,640]{3,2,1,0:T(8,128)(2,1)S(1)}, bf16[2,3,320,640]{3,2,1,0:T(8,128)(2,1)}, u32[]{:S(2)}) copy-start(bf16[2,3,320,640]{3,2,1,0:T(8,128)(2,1)} %weights.9) | copy-start | bytes 7372804
  10.8 3.3 %copy-start.6 = (s32[96,2560]{1,0:T(8,128)S(1)}, s32[96,2560]{1,0:T(8,128)}, u32[]{:S(2)}) copy-start(s32[96,2560]{1,0:T(8,128)} %out_bits.1) | copy-start | bytes 2949124
  10.9 3.3 %copy-start.16 = (s32[24,2560]{1,0:T(8,128)S(1)}, s32[24,2560]{1,0:T(8,128)}, u32[]{:S(2)}) copy-start(s32[24,2560]{1,0:T(8,128)} %in_bits.1) | copy-start | bytes 737284
  10.9 3.3 %copy-start.17 = (s32[96,640]{1,0:T(8,128)S(1)}, s32[96,640]{1,0:T(8,128)}, u32[]{:S(2)}) copy-start(s32[96,640]{1,0:T(8,128)} %mix_bits.1) | copy-start | bytes 737284
  10.9 3.3 %copy-start.20 = (bf16[24,2560]{1,0:T(8,128)(2,1)S(1)}, bf16[24,2560]{1,0:T(8,128)(2,1)}, u32[]{:S(2)}) copy-start(bf16[24,2560]{1,0:T(8,128)(2,1)} %tokens) | copy-start | bytes 368644
  11.1 46.5 %collective-permute-start.5 = (bf16[2,2,320,640]{3,2,1,0:T(8,128)(2,1)S(1)}, bf16[2,2,320,640]{3,2,1,0:T(8,128)(2,1)S(1)}, u32[]{:S(2)}, u32[]{:S(2)}) collective-permute-start(bf16[2,2,320,640]{3,2,1,0:T(8,128)(2,1)S(1)} %shard_map.91), channel_id=1, source_target_pairs={{0,4},{4,0},{8,12},{12,8},{16,20},{20,16},{24,28},{28,24},{1,5},{5... | collective-permute-start | bytes 4915208 | tf_op jit(solution)/shard_map/ppermute | solution.py:353
  15.6 42.0 %copy-start.10 = (bf16[8,24,640]{2,1,0:T(8,128)(2,1)}, bf16[8,24,640]{2,1,0:T(8,128)(2,1)S(1)}, u32[]{:S(2)}) copy-start(bf16[8,24,640]{2,1,0:T(8,128)(2,1)S(1)} %get-tuple-element.37.refs_0_) | copy-start | bytes 737284
  15.6 18.0 %collective-permute-start = (bf16[8,24,640]{2,1,0:T(8,128)(2,1)S(1)}, bf16[8,24,640]{2,1,0:T(8,128)(2,1)S(1)}, u32[]{:S(2)}, u32[]{:S(2)}) collective-permute-start(bf16[8,24,640]{2,1,0:T(8,128)(2,1)S(1)} %get-tuple-element.38), channel_id=1, source_target_pairs={{0,8},{4,12},{8,0},{12,4},{16,24},{20,28},{24,16},{28,20},{1,9},{5... | collective-permute-start | bytes 737288 | tf_op jit(solution)/shard_map/ppermute | solution.py:356
  17.5 29.1 %collective-permute-start.1 = (bf16[8,24,640]{2,1,0:T(8,128)(2,1)S(1)}, bf16[8,24,640]{2,1,0:T(8,128)(2,1)S(1)}, u32[]{:S(2)}, u32[]{:S(2)}) collective-permute-start(bf16[8,24,640]{2,1,0:T(8,128)(2,1)S(1)} %get-tuple-element.39), channel_id=1, source_target_pairs={{0,16},{4,20},{8,24},{12,28},{16,0},{20,4},{24,8},{28,12},{1,17},{... | collective-permute-start | bytes 737288 | tf_op jit(solution)/shard_map/ppermute | solution.py:356
  20.1 29.1 %collective-permute-start.2 = (bf16[8,24,640]{2,1,0:T(8,128)(2,1)S(1)}, bf16[8,24,640]{2,1,0:T(8,128)(2,1)S(1)}, u32[]{:S(2)}, u32[]{:S(2)}) collective-permute-start(bf16[8,24,640]{2,1,0:T(8,128)(2,1)S(1)} %get-tuple-element.40), channel_id=1, source_target_pairs={{0,24},{4,28},{8,16},{12,20},{16,8},{20,12},{24,0},{28,4},{1,25},{... | collective-permute-start | bytes 737288 | tf_op jit(solution)/shard_map/ppermute | solution.py:356
  33.6 23.9 %copy-start.7 = (bf16[8,24,640]{2,1,0:T(8,128)(2,1)}, bf16[8,24,640]{2,1,0:T(8,128)(2,1)S(1)}, u32[]{:S(2)}) copy-start(bf16[8,24,640]{2,1,0:T(8,128)(2,1)S(1)} %collective-permute-done.refs_1_) | copy-start | bytes 737284
  46.6 11.0 %copy-start.8 = (bf16[8,24,640]{2,1,0:T(8,128)(2,1)}, bf16[8,24,640]{2,1,0:T(8,128)(2,1)S(1)}, u32[]{:S(2)}) copy-start(bf16[8,24,640]{2,1,0:T(8,128)(2,1)S(1)} %collective-permute-done.1.refs_2_) | copy-start | bytes 737284
  49.2 1.7 copy-start.9
  49.2 6.3 %collective-permute-start.3 = (bf16[4,2,24,640]{3,2,1,0:T(8,128)(2,1)S(1)}, bf16[4,2,24,640]{3,2,1,0:T(8,128)(2,1)S(1)}, u32[]{:S(2)}, u32[]{:S(2)}) collective-permute-start(bf16[4,2,24,640]{3,2,1,0:T(8,128)(2,1)S(1)} %shard_map.94.own), channel_id=1, source_target_pairs={{0,2},{1,3},{2,0},{3,1},{4,6},{5,7},{6,4},{7,5},{8,10},{9,11},{10,... | collective-permute-start | bytes 737288 | tf_op jit(solution)/shard_map/ppermute | solution.py:359
  55.6 1.9 %collective-permute-start.4 = (bf16[2,4,2,24,640]{4,3,2,1,0:T(8,128)(2,1)S(1)}, bf16[2,4,2,24,640]{4,3,2,1,0:T(8,128)(2,1)S(1)}, u32[]{:S(2)}, u32[]{:S(2)}) collective-permute-start(bf16[2,4,2,24,640]{4,3,2,1,0:T(8,128)(2,1)S(1)} %shard_map.95.own), channel_id=1, source_target_pairs={{0,1},{1,0},{2,3},{3,2},{4,5},{5,4},{6,7},{7,6},{8,9},{9,8},{10,11... | collective-permute-start | bytes 1474568 | tf_op jit(solution)/shard_map/ppermute | solution.py:359
  57.6 1.2 copy-start.2
  58.8 21.7 %collective-permute-start.8 = (bf16[320,640]{1,0:T(8,128)(2,1)}, bf16[320,640]{1,0:T(8,128)(2,1)}, u32[]{:S(2)}, u32[]{:S(2)}) collective-permute-start(bf16[320,640]{1,0:T(8,128)(2,1)} %get-tuple-element.49), channel_id=1, source_target_pairs={{0,4},{4,0},{8,12},{12,8},{16,20},{20,16},{24,28},{28,24},{1,5},{5... | collective-permute-start | bytes 1228808 | tf_op jit(solution)/shard_map/ppermute | solution.py:353
  65.7 1.4 copy-start.3
  67.2 1.4 copy-start.4
  71.7 19.3 %collective-permute-start.7 = (bf16[1152,128]{1,0:T(8,128)(2,1)S(1)}, bf16[1152,128]{1,0:T(8,128)(2,1)S(1)}, u32[]{:S(2)}, u32[]{:S(2)}) collective-permute-start(bf16[1152,128]{1,0:T(8,128)(2,1)S(1)} %get-tuple-element.41), channel_id=1, source_target_pairs={{0,8},{4,12},{8,0},{12,4},{16,24},{20,28},{24,16},{28,20},{1,9},{5... | collective-permute-start | bytes 884744 | tf_op jit(solution)/shard_map/ppermute | solution.py:356
  80.5 20.1 %collective-permute-start.10 = (bf16[320,640]{1,0:T(8,128)(2,1)}, bf16[320,640]{1,0:T(8,128)(2,1)}, u32[]{:S(2)}, u32[]{:S(2)}) collective-permute-start(bf16[320,640]{1,0:T(8,128)(2,1)} %get-tuple-element.53), channel_id=1, source_target_pairs={{0,4},{4,0},{8,12},{12,8},{16,20},{20,16},{24,28},{28,24},{1,5},{5... | collective-permute-start | bytes 1228808 | tf_op jit(solution)/shard_map/ppermute | solution.py:353
  85.9 5.9 %copy-start.18 = (f32[384,128]{1,0:T(8,128)}, f32[384,128]{1,0:T(8,128)S(1)}, u32[]{:S(2)}) copy-start(f32[384,128]{1,0:T(8,128)S(1)} %get-tuple-element.44.keep_two) | copy-start | bytes 589828
  85.9 15.9 %collective-permute-start.6 = (bf16[1152,128]{1,0:T(8,128)(2,1)}, bf16[1152,128]{1,0:T(8,128)(2,1)}, u32[]{:S(2)}, u32[]{:S(2)}) collective-permute-start(bf16[1152,128]{1,0:T(8,128)(2,1)} %get-tuple-element.45), channel_id=1, source_target_pairs={{0,8},{4,12},{8,0},{12,4},{16,24},{20,28},{24,16},{28,20},{1,9},{5... | collective-permute-start | bytes 884744 | tf_op jit(solution)/shard_map/ppermute | solution.py:356
  92.5 9.2 %collective-permute-start.9 = (bf16[768,128]{1,0:T(8,128)(2,1)}, bf16[768,128]{1,0:T(8,128)(2,1)}, u32[]{:S(2)}, u32[]{:S(2)}) collective-permute-start(bf16[768,128]{1,0:T(8,128)(2,1)} %get-tuple-element.51), channel_id=1, source_target_pairs={{0,16},{4,20},{8,24},{12,28},{16,0},{20,4},{24,8},{28,12},{1,17},{... | collective-permute-start | bytes 589832 | tf_op jit(solution)/shard_map/ppermute | solution.py:356
  96.8 4.9 %copy-start.19 = (f32[384,128]{1,0:T(8,128)S(1)}, f32[384,128]{1,0:T(8,128)}, u32[]{:S(2)}) copy-start(f32[384,128]{1,0:T(8,128)} %copy-done.18) | copy-start | bytes 589828
  96.8 6.9 %copy-start.5 = (bf16[12,96,640]{2,1,0:T(8,128)(2,1)S(1)}, bf16[12,96,640]{2,1,0:T(8,128)(2,1)}, u32[]{:S(2)}) copy-start(bf16[12,96,640]{2,1,0:T(8,128)(2,1)} %all-gather.3.cloned.1.call-done) | copy-start | bytes 4423684
  101.7 1.0 copy-start.13
  106.9 6.0 %copy-start.15 = (f32[768,128]{1,0:T(8,128)S(1)}, f32[768,128]{1,0:T(8,128)}, u32[]{:S(2)}) copy-start(f32[768,128]{1,0:T(8,128)} %copy-done.14) | copy-start | bytes 1179652
  106.9 15.0 %copy-start.21 = (f32[640]{0:T(1024)S(1)}, f32[640]{0:T(1024)}, u32[]{:S(2)}) copy-start(f32[640]{0:T(1024)} %param.14) | copy-start | bytes 7684
  106.9 15.8 %collective-permute-start.11 = (bf16[960,128]{1,0:T(8,128)(2,1)S(1)}, bf16[960,128]{1,0:T(8,128)(2,1)S(1)}, u32[]{:S(2)}, u32[]{:S(2)}) collective-permute-start(bf16[960,128]{1,0:T(8,128)(2,1)S(1)} %get-tuple-element.59), channel_id=1, source_target_pairs={{0,8},{4,12},{8,0},{12,4},{16,24},{20,28},{24,16},{28,20},{1,9},{5... | collective-permute-start | bytes 737288 | tf_op jit(solution)/shard_map/ppermute | solution.py:356
  110.8 12.7 %copy-start.23 = (bf16[2,640,320]{1,2,0:T(8,128)(2,1)S(1)}, bf16[2,640,320]{1,2,0:T(8,128)(2,1)}, u32[]{:S(2)}) copy-start(bf16[2,640,320]{1,2,0:T(8,128)(2,1)} %param.15) | copy-start | bytes 2457604
  110.8 19.8 %copy-start.22 = (f32[640]{0:T(1024)S(1)}, f32[640]{0:T(1024)}, u32[]{:S(2)}) copy-start(f32[640]{0:T(1024)} %param.13) | copy-start | bytes 7684
  110.8 11.2 %collective-permute-start.13 = (bf16[768,128]{1,0:T(8,128)(2,1)S(1)}, bf16[768,128]{1,0:T(8,128)(2,1)S(1)}, u32[]{:S(2)}, u32[]{:S(2)}) collective-permute-start(bf16[768,128]{1,0:T(8,128)(2,1)S(1)} %get-tuple-element.62), channel_id=1, source_target_pairs={{0,16},{4,20},{8,24},{12,28},{16,0},{20,4},{24,8},{28,12},{1,17},{... | collective-permute-start | bytes 589832 | tf_op jit(solution)/shard_map/ppermute | solution.py:356
  113.9 11.2 %collective-permute-start.15 = (bf16[768,128]{1,0:T(8,128)(2,1)S(1)}, bf16[768,128]{1,0:T(8,128)(2,1)S(1)}, u32[]{:S(2)}, u32[]{:S(2)}) collective-permute-start(bf16[768,128]{1,0:T(8,128)(2,1)S(1)} %shard_map.103.values_a), channel_id=1, source_target_pairs={{0,4},{4,0},{8,12},{12,8},{16,20},{20,16},{24,28},{28,24},{1,5},{5... | collective-permute-start | bytes 589832 | tf_op jit(solution)/shard_map/ppermute | solution.py:353
  122.7 7.9 %collective-permute-start.14 = (bf16[768,128]{1,0:T(8,128)(2,1)S(1)}, bf16[768,128]{1,0:T(8,128)(2,1)S(1)}, u32[]{:S(2)}, u32[]{:S(2)}) collective-permute-start(bf16[768,128]{1,0:T(8,128)(2,1)S(1)} %shard_map.104.keys_a), channel_id=1, source_target_pairs={{0,4},{4,0},{8,12},{12,8},{16,20},{20,16},{24,28},{28,24},{1,5},{5... | collective-permute-start | bytes 589832 | tf_op jit(solution)/shard_map/ppermute | solution.py:353
  122.9 6.4 %collective-permute-start.12 = (bf16[480,128]{1,0:T(8,128)(2,1)S(1)}, bf16[480,128]{1,0:T(8,128)(2,1)S(1)}, u32[]{:S(2)}, u32[]{:S(2)}) collective-permute-start(bf16[480,128]{1,0:T(8,128)(2,1)S(1)} %get-tuple-element.61), channel_id=1, source_target_pairs={{0,16},{4,20},{8,24},{12,28},{16,0},{20,4},{24,8},{28,12},{1,17},{... | collective-permute-start | bytes 368648 | tf_op jit(solution)/shard_map/ppermute | solution.py:356
  123.5 21.3 %collective-permute-start.19 = (bf16[2,320,640]{2,1,0:T(8,128)(2,1)S(1)}, bf16[2,320,640]{2,1,0:T(8,128)(2,1)S(1)}, u32[]{:S(2)}, u32[]{:S(2)}) collective-permute-start(bf16[2,320,640]{2,1,0:T(8,128)(2,1)S(1)} %bitcast.79), channel_id=1, source_target_pairs={{0,4},{4,0},{8,12},{12,8},{16,20},{20,16},{24,28},{28,24},{1,5},{5... | collective-permute-start | bytes 2457608 | tf_op jit(solution)/shard_map/ppermute | solution.py:353
  132.1 9.2 %collective-permute-start.18 = (bf16[480,128]{1,0:T(8,128)(2,1)S(1)}, bf16[480,128]{1,0:T(8,128)(2,1)S(1)}, u32[]{:S(2)}, u32[]{:S(2)}) collective-permute-start(bf16[480,128]{1,0:T(8,128)(2,1)S(1)} %shard_map.105), channel_id=1, source_target_pairs={{0,24},{4,28},{8,16},{12,20},{16,8},{20,12},{24,0},{28,4},{1,25},{... | collective-permute-start | bytes 368648 | tf_op jit(solution)/shard_map/ppermute | solution.py:356
  132.1 9.0 %collective-permute-start.17 = (bf16[480,128]{1,0:T(8,128)(2,1)S(1)}, bf16[480,128]{1,0:T(8,128)(2,1)S(1)}, u32[]{:S(2)}, u32[]{:S(2)}) collective-permute-start(bf16[480,128]{1,0:T(8,128)(2,1)S(1)} %shard_map.105), channel_id=1, source_target_pairs={{0,16},{4,20},{8,24},{12,28},{16,0},{20,4},{24,8},{28,12},{1,17},{... | collective-permute-start | bytes 368648 | tf_op jit(solution)/shard_map/ppermute | solution.py:356
  132.2 8.0 %collective-permute-start.16 = (bf16[480,128]{1,0:T(8,128)(2,1)S(1)}, bf16[480,128]{1,0:T(8,128)(2,1)S(1)}, u32[]{:S(2)}, u32[]{:S(2)}) collective-permute-start(bf16[480,128]{1,0:T(8,128)(2,1)S(1)} %shard_map.105), channel_id=1, source_target_pairs={{0,8},{4,12},{8,0},{12,4},{16,24},{20,28},{24,16},{28,20},{1,9},{5... | collective-permute-start | bytes 368648 | tf_op jit(solution)/shard_map/ppermute | solution.py:356
  146.9 2.6 %collective-permute-start.20 = (bf16[2,4,2,24,640]{4,3,1,2,0:T(8,128)(2,1)S(1)}, bf16[2,4,2,24,640]{4,3,1,2,0:T(8,128)(2,1)S(1)}, u32[]{:S(2)}, u32[]{:S(2)}) collective-permute-start(bf16[2,4,2,24,640]{4,3,1,2,0:T(8,128)(2,1)S(1)} %slice.180), channel_id=1, source_target_pairs={{0,1},{1,0},{2,3},{3,2},{4,5},{5,4},{6,7},{7,6},{8,9},{9,8},{10,11... | collective-permute-start | bytes 1474568 | tf_op jit(solution)/shard_map/ppermute | solution.py:359
  149.7 5.8 %collective-permute-start.21 = (bf16[4,24,640]{2,1,0:T(8,128)(2,1)S(1)}, bf16[4,24,640]{2,1,0:T(8,128)(2,1)S(1)}, u32[]{:S(2)}, u32[]{:S(2)}) collective-permute-start(bf16[4,24,640]{2,1,0:T(8,128)(2,1)S(1)} %fusion.17), channel_id=1, source_target_pairs={{0,2},{1,3},{2,0},{3,1},{4,6},{5,7},{6,4},{7,5},{8,10},{9,11},{10,... | collective-permute-start | bytes 368648 | tf_op jit(solution)/shard_map/ppermute | solution.py:359
  155.6 5.8 %collective-permute-start.24 = (bf16[24,640]{1,0:T(8,128)(2,1)S(1)}, bf16[24,640]{1,0:T(8,128)(2,1)S(1)}, u32[]{:S(2)}, u32[]{:S(2)}) collective-permute-start(bf16[24,640]{1,0:T(8,128)(2,1)S(1)} %get-tuple-element.74), channel_id=1, source_target_pairs={{0,24},{4,28},{8,16},{12,20},{16,8},{20,12},{24,0},{28,4},{1,25},{... | collective-permute-start | bytes 92168 | tf_op jit(solution)/shard_map/ppermute | solution.py:356
  155.7 5.7 %collective-permute-start.23 = (bf16[24,640]{1,0:T(8,128)(2,1)S(1)}, bf16[24,640]{1,0:T(8,128)(2,1)S(1)}, u32[]{:S(2)}, u32[]{:S(2)}) collective-permute-start(bf16[24,640]{1,0:T(8,128)(2,1)S(1)} %get-tuple-element.75), channel_id=1, source_target_pairs={{0,16},{4,20},{8,24},{12,28},{16,0},{20,4},{24,8},{28,12},{1,17},{... | collective-permute-start | bytes 92168 | tf_op jit(solution)/shard_map/ppermute | solution.py:356
  156.8 5.1 %collective-permute-start.22 = (bf16[24,640]{1,0:T(8,128)(2,1)S(1)}, bf16[24,640]{1,0:T(8,128)(2,1)S(1)}, u32[]{:S(2)}, u32[]{:S(2)}) collective-permute-start(bf16[24,640]{1,0:T(8,128)(2,1)S(1)} %get-tuple-element.76), channel_id=1, source_target_pairs={{0,8},{4,12},{8,0},{12,4},{16,24},{20,28},{24,16},{28,20},{1,9},{5... | collective-permute-start | bytes 92168 | tf_op jit(solution)/shard_map/ppermute | solution.py:356
  (2 other events, 1.5 us)
Sparse Core Ops, SparseCore 0:
  9.3 56.4 all-gather.2

commit v2 on v1

--- a/solution.py
+++ b/solution.py
@@ -160,31 +160,34 @@
         signs[part] = jnp.concatenate(pieces, axis=0).astype(bf)
 
 
-def prepare_kernel(
-    team, place, tokens, in_bits, out_bits, mix_bits, weights, query_a, query_b, *refs
-):
+def prepare_kernel(place, tokens, in_bits, *blocks):
+    wide = tokens.shape[1] // len(blocks)
+    for k, block in enumerate(blocks):
+        cut = lanes(place[0] ^ k, wide)
+        plain = tokens[:, cut]
+        sign = (2 * in_bits[:, cut] - 1).astype(jnp.float32)
+        block[0] = plain
+        block[1] = (plain.astype(jnp.float32) * sign).astype(bf)
+
+
+def late_signs_kernel(team, place, out_bits, mix_bits, weights, query_weights, *refs):
     blocks, sems = refs[:-1], refs[-1]
     copies = [
-        pltpu.make_async_copy(weights.at[m, 0], out, sems.at[m])
-        for m, out in ((0, query_a), (1, query_b))
+        pltpu.make_async_copy(weights.at[m, 0], query_weights.at[m], sems.at[m]) for m in (0, 1)
     ]
     for copy in copies:
         copy.start()
     z, u = place[0], place[2]
-    own_rows = tokens.shape[0]
-    wide = tokens.shape[1] // len(blocks)
+    wide = out_bits.shape[1] // len(blocks)
+    own_rows = blocks[0].shape[1]
     mix = [part.astype(bf) for part in sign_pieces(mix_bits, u, team)]
     for k, block in enumerate(blocks):
         cut = lanes(z ^ k, wide)
-        plain = tokens[:, cut]
-        sign = (2 * in_bits[:, cut] - 1).astype(jnp.float32)
-        block[0] = plain
-        block[1] = (plain.astype(jnp.float32) * sign).astype(bf)
         for i, r in enumerate((0, 2)):
             bits = out_bits[pl.ds(pl.multiple_of((u ^ r) * own_rows, 8), own_rows), cut]
-            block[2 + i] = (2 * bits - 1).astype(jnp.float32).astype(bf)
+            block[i] = (2 * bits - 1).astype(jnp.float32).astype(bf)
         for r in range(team):
-            block[4 + r] = mix[r]
+            block[2 + r] = mix[r]
     for copy in copies:
         copy.wait()
 
@@ -208,41 +211,24 @@
             rows[m, at : at + 4 * piece] = jnp.concatenate(parts, axis=0).astype(bf)
 
 
-def sum_kernel(total, taken, out):
-    out[...] = (total[...] + taken[...].astype(jnp.float32)).astype(bf)
-
-
 def project_kernel(
-    part, size, place, rows, weights, partner_0, partner_1, all_signs,
-    send, keep_own, keep_two, held, total, signs, sems, sign_sems,
+    parts, size, place, rows, weights, partner, signs_0, signs_2, signs_13,
+    send, keep_own, keep_two, held, total, sems,
 ):
     z, x = place[0], place[1]
     slab = weights.shape[2]
-    partner = (partner_0, partner_1)
-    if part:
-        partner = (partner_0.at[0, part - 1], partner_0.at[1, part - 1])
     own = pl.ds(pl.multiple_of(x * slab, 64), slab)
     other = pl.ds(pl.multiple_of((1 - x) * slab, 64), slab)
     depth = rows.shape[1] // size
+    half = depth * size
     copies = []
-    for m in (0, 1):
-        copies.append(
-            pltpu.make_async_copy(weights.at[m, part], held.at[m, own], sems.at[m, 0])
-        )
-        copies.append(pltpu.make_async_copy(partner[m], held.at[m, other], sems.at[m, 1]))
-    for j in range(depth):
-        copies.append(
-            pltpu.make_async_copy(all_signs.at[z ^ j, part], signs.at[j], sign_sems.at[j])
-        )
+    for i, part in enumerate(parts):
+        for m in (0, 1):
+            near, far = weights.at[m, part], partner.at[m, i]
+            copies.append(pltpu.make_async_copy(near, held.at[i, m, own], sems.at[i, m, 0]))
+            copies.append(pltpu.make_async_copy(far, held.at[i, m, other], sems.at[i, m, 1]))
     for copy in copies:
         copy.start()
-    for copy in copies:
-        copy.wait()
-    total[...] = dot32(rows[1], held[1])
-    plain = dot32(rows[0], held[0])
-    for j in range(depth):
-        cut = slice(j * size, (j + 1) * size)
-        total[cut] = plain[cut] + signs[j].astype(jnp.float32) * total[cut]
 
     def block(j, head):
         return total[j * size : (j + 1) * size, lanes(head, HEAD)]
@@ -255,38 +241,54 @@
     def rest(target, start, j):
         target[start : start + size] = block(j, depth).astype(target.dtype)
 
-    half = depth * size
-    main(keep_own, 0, 0)
-    main(keep_two, 0, 2)
-    main(send, 0, 1)
-    if part:
-        main(send, half, 3)
+    for i, part in enumerate(parts):
+        for copy in copies[4 * i : 4 * i + 4]:
+            copy.wait()
+        total[...] = dot32(rows[1], held[i, 1])
+        plain = dot32(rows[0], held[i, 0])
+        signs = (signs_0[part], signs_13[0, part], signs_2[part], signs_13[1, part])
         for j in range(depth):
-            rest(send, 2 * half + (j ^ 1) * size, j)
-            rest(keep_own, half + j * size, j)
-    else:
-        rest(send, half, 1)
-        main(send, half + size, 3)
-        rest(send, 2 * half + size, 3)
-        rest(keep_own, half, 0)
-        rest(keep_two, half, 2)
+            cut = slice(j * size, (j + 1) * size)
+            total[cut] = plain[cut] + signs[j].astype(jnp.float32) * total[cut]
+        if part:
+            main(send, 3 * half * i, 1)
+            main(send, 3 * half * i + half, 3)
+            main(keep_own, 2 * half * i, 0)
+            main(keep_two, half * i, 2)
+            for j in range(depth):
+                rest(send, 3 * half * i + 2 * half + (j ^ 1) * size, j)
+                rest(keep_own, 2 * half * i + half + j * size, j)
+        else:
+            main(send, 0, 1)
+            rest(send, half, 1)
+            main(send, half + size, 3)
+            rest(send, 2 * half + size, 3)
+            main(keep_own, 0, 0)
+            rest(keep_own, half, 0)
+            main(keep_two, 0, 2)
+            rest(keep_two, half, 2)
 
 
 def middle_kernel(size, keep_own, keep_two, taken, send, total):
-    half = keep_two.shape[0]
-    if keep_own.shape[0] == half:
-        total[...] = keep_own[...] + taken[:half].astype(jnp.float32)
-        send[...] = (keep_two[...] + taken[half:].astype(jnp.float32)).astype(bf)
+    count = keep_two.shape[0]
+    if keep_own.shape[0] == count:
+        total[...] = keep_own[...] + taken[:count].astype(jnp.float32)
+        send[...] = (keep_two[...] + taken[count:].astype(jnp.float32)).astype(bf)
         return
-    total[:half] = keep_own[:half] + taken[:half].astype(jnp.float32)
-    send[:half] = (keep_two[...] + taken[half : 2 * half].astype(jnp.float32)).astype(bf)
-    for j in range(half // size):
-        cut = slice(half + j * size, half + (j + 1) * size)
-        got = taken[half + cut.start : half + cut.stop].astype(jnp.float32)
-        value = keep_own[cut] + got
-        total[cut] = value
-        at = half + (j ^ 2) * size
-        send[at : at + size] = value.astype(bf)
+    half = count // 2
+    for i in (0, 1):
+        base, got = 2 * half * i, 3 * half * i
+        first = slice(base, base + half)
+        total[first] = keep_own[first] + taken[got : got + half].astype(jnp.float32)
+        far = keep_two[half * i : half * i + half]
+        send[first] = (far + taken[got + half : got + 2 * half].astype(jnp.float32)).astype(bf)
+        for j in range(half // size):
+            cut = slice(base + half + j * size, base + half + (j + 1) * size)
+            at = got + 2 * half + j * size
+            value = keep_own[cut] + taken[at : at + size].astype(jnp.float32)
+            total[cut] = value
+            at = base + half + (j ^ 2) * size
+            send[at : at + size] = value.astype(bf)
 
 
 def norm_rows(values, gain_row):
@@ -295,27 +297,26 @@
     return (wide * inverse_rms * gain_row).astype(bf)
 
 
-def key_kernel(half, place, total, taken, gain, keys):
+def key_value_kernel(half, place, total, taken, gain, out):
     keep = (total[...] + taken[...].astype(jnp.float32)).astype(bf)
     heads = gain.shape[0]
-    keys[:half] = norm_rows(keep[:half], gain[pl.ds(place[0], 1), :])
-    keys[half:] = norm_rows(keep[half:], gain[heads - 1 : heads, :])
-
-
-def attend_kernel(
-    half, place, total, taken, gain, keys_a, keys_b, values_a, values_b, out
-):
+    out[:half] = norm_rows(keep[:half], gain[pl.ds(place[0], 1), :])
+    out[half : 2 * half] = norm_rows(keep[half : 2 * half], gain[heads - 1 : heads, :])
+    out[2 * half :] = keep[2 * half :]
+
+
+def attend_kernel(half, place, total, taken, gain, own, partner, out):
     keep = (total[...] + taken[...].astype(jnp.float32)).astype(bf)
     heads = gain.shape[0]
 
     def attend(queries, cut):
         score_scale = 1.0 / math.sqrt(HEAD)
         totals, sums = 0.0, 0.0
-        for keys, values in ((keys_a, values_a), (keys_b, values_b)):
-            scores = dot32_t(queries, keys[cut]) * score_scale
+        for both in (own, partner):
+            scores = dot32_t(queries, both[cut]) * score_scale
             weights = jnp.exp(scores).astype(bf)
             totals = totals + jnp.sum(weights.astype(jnp.float32), axis=1, keepdims=True)
-            sums = sums + dot32(weights, values[cut])
+            sums = sums + dot32(weights, both[2 * half + cut.start : 2 * half + cut.stop])
         return (sums / totals).astype(bf)
 
     first = norm_rows(keep[:half], gain[pl.ds(place[0], 1), :])
@@ -367,46 +368,53 @@
     )(qkv_weights)
     partner_early = swap_x(early)
 
+    blocks = call(
+        prepare_kernel,
+        [shape(2, own_rows, 2 * slab)] * depth, [VMEM] * depth, [SMEM] + [VMEM] * 2,
+    )(place, after(tokens, early), in_bits)
+    got = [blocks[0]] + [swap_z(blocks[k], k) for k in steps if k]
+
     sign_bits = jnp.transpose(qkv_bits, (1, 0, 2))
     sign_own = call(
         functools.partial(sign_kernel, team), shape(3, size, columns), VMEM, [SMEM, VMEM]
-    )(place, sign_bits)
-    all_signs = lax.all_gather(
-        sign_own, "blk", axis=0, axis_index_groups=[[2 * i + j for i in steps] for j in (0, 1)]
-    )
-
-    query_a, query_b, *blocks = call(
-        functools.partial(prepare_kernel, team),
-        [shape(slab, columns)] * 2 + [shape(4 + team, own_rows, 2 * slab)] * depth,
-        [ANY] * 2 + [VMEM] * depth,
-        [SMEM] + [VMEM] * 4 + [ANY],
-        [pltpu.SemaphoreType.DMA((2,))],
-    )(place, after(tokens, early, sign_own), in_bits, out_bits, mix_bits, qkv_weights)
-    got = [blocks[0]] + [swap_z(blocks[k], k) for k in steps if k]
+    )(place, after(sign_bits, blocks[0]))
+    sign_two = swap_z(sign_own, 2)
+    sign_pair = call(pair_kernel, shape(2, 3, size, columns), VMEM, [VMEM] * 2)(sign_own, sign_two)
+    signs = (sign_own, sign_two, swap_z(sign_pair, 1))
+
     held_shape = (depth, 2, own_rows, 2 * slab)
     held = call(stack_kernel, shape(*held_shape), VMEM, [VMEM] * depth)(*got)
     held = call(pair_kernel, shape(2, *held_shape), VMEM, [VMEM] * 2)(held, swap_u(held, 2))
     rows = call(rows_kernel, shape(2, half, 2 * slab), VMEM, [VMEM] * 2)(held, swap_u(held, 1))
 
-    query_a = swap_x(after(query_a, partner_early, rows))
-    query_b = swap_x(after(query_b, query_a))
-    partner = {2: [partner_early] * 2, 1: [partner_early] * 2, 0: [query_a, query_b]}
-
-    def project(part, rows):
-        counts = (3 * half, 2 * half, half) if part else (2 * (half + size),) + (half + size,) * 2
+    query_weights, *late = call(
+        functools.partial(late_signs_kernel, team),
+        [shape(2, slab, columns)] + [shape(2 + team, own_rows, 2 * slab)] * depth,
+        [ANY] + [VMEM] * depth,
+        [SMEM] + [VMEM] * 2 + [ANY],
+        [pltpu.SemaphoreType.DMA((2,))],
+    )(place, after(out_bits, sign_own), mix_bits, qkv_weights)
+    partner_query = swap_x(after(query_weights, partner_early, rows, sign_pair))
+    out_t = jnp.transpose(out_weights, (0, 2, 1))
+    out_partner = swap_x(after(out_t, partner_query))
+
+    def project(parts, rows, partner):
+        whole = len(parts)
+        count = half + size
+        counts = (3 * half * whole, 2 * half * whole, half * whole)
+        if parts == (0,):
+            counts = (2 * count, count, count)
         return call(
-            functools.partial(project_kernel, part, size),
+            functools.partial(project_kernel, parts, size),
             [shape(counts[0], HEAD)] + [shape(count, HEAD, dtype=f32) for count in counts[1:]],
             [VMEM] * 3,
-            [SMEM, VMEM] + [ANY] * 4,
+            [SMEM, VMEM, ANY, ANY] + [VMEM] * 3,
             [
-                pltpu.VMEM((2, 2 * slab, columns), bf),
+                pltpu.VMEM((whole, 2, 2 * slab, columns), bf),
                 pltpu.VMEM((half, columns), f32),
-                pltpu.VMEM((depth, size, columns), bf),
-                pltpu.SemaphoreType.DMA((2, 2)),
-                pltpu.SemaphoreType.DMA((depth,)),
+                pltpu.SemaphoreType.DMA((whole, 2, 2)),
             ],
-        )(place, rows, qkv_weights, *partner[part], all_signs)
+        )(place, rows, qkv_weights, partner, *signs)
 
     def middle(keep_own, keep_two, taken):
         count = keep_own.shape[0]
@@ -417,37 +425,25 @@
             [VMEM] * 3,
         )(keep_own, keep_two, taken)
 
-    value_send, keep_own, keep_two = project(2, rows)
-    key_send, key_own, key_two = project(1, after(rows, value_send))
-    taken = after(swap_z(value_send, 1), key_send, query_a)
-    send, value_total = middle(keep_own, keep_two, taken)
-    value_last = swap_z(send, 2)
-    taken = after(swap_z(key_send, 1), value_last, query_b)
-    send, key_total = middle(key_own, key_two, taken)
-    key_last = swap_z(send, 2)
-    query_send, query_own, query_two = project(0, after(rows, key_total))
-    taken = swap_z(query_send, 1)
-    values = call(sum_kernel, shape(2 * half, HEAD), VMEM, [VMEM] * 2)(
-        value_total, after(value_last, query_send)
-    )
-    values_partner = swap_x(values)
-    keys = call(
-        functools.partial(key_kernel, half), shape(2 * half, HEAD), VMEM, [SMEM] + [VMEM] * 3
-    )(place, key_total, after(key_last, values), gain_key.reshape(heads, HEAD))
-    keys_partner = swap_x(keys)
-    send, query_total = middle(query_own, query_two, taken)
-    out_t = jnp.transpose(out_weights, (0, 2, 1))
-    out_partner = swap_x(after(out_t, keys, query_total))
-
+    both_send, both_own, both_two = project((1, 2), rows, partner_early)
+    taken = swap_z(both_send, 1)
+    late = [late[0]] + [swap_z(after(late[k], signs[2]), k) for k in steps if k]
+    query_send, query_own, query_two = project(
+        (0,), after(rows, both_send), partner_query.reshape(2, 1, slab, columns)
+    )
+    query_taken = swap_z(query_send, 1)
+    send, both_total = middle(both_own, both_two, after(taken, query_send, *late[1:]))
+    both_last = swap_z(send, 2)
+    send, query_total = middle(query_own, query_two, after(query_taken, both_total))
+    query_last = swap_z(send, 2)
+    both = call(
+        functools.partial(key_value_kernel, half),
+        shape(4 * half, HEAD), VMEM, [SMEM] + [VMEM] * 3,
+    )(place, both_total, after(both_last, query_total), gain_key.reshape(heads, HEAD))
     done = call(
         functools.partial(attend_kernel, half),
-        shape(half + size, HEAD),
-        VMEM,
-        [SMEM] + [VMEM] * 7,
-    )(
-        place, query_total, swap_z(send, 2), gain_query.reshape(heads, HEAD),
-        keys, keys_partner, values, values_partner,
-    )
+        shape(half + size, HEAD), VMEM, [SMEM] + [VMEM] * 5,
+    )(place, query_total, query_last, gain_query.reshape(heads, HEAD), both, swap_x(both))
 
     by_head, last_head = [], []
     for k in steps:
@@ -463,7 +459,7 @@
         ] + [lax.slice_in_dim(value, depth * HEAD, heads * HEAD, axis=axis)]
         return jnp.concatenate(parts, axis=axis)
 
-    mix = relative(jnp.concatenate([g[4:].reshape(size, columns) for g in got], axis=0), 1)
+    mix = relative(jnp.concatenate([g[2:].reshape(size, columns) for g in late], axis=0), 1)
     attended_flipped = attended * mix
     first = jnp.where(x == 0, out_t, out_partner)
     second = jnp.where(x == 0, out_partner, out_t)
@@ -473,7 +469,7 @@
     ).astype(bf)
     partial = partial.reshape(2, depth, team, own_rows, 2 * slab)
     summed = partial[:, :, 0::2].astype(f32) + swap_u(partial[:, :, 1::2], 1).astype(f32)
-    out_signs = jnp.stack([g[2:4] for g in got]).astype(f32)
+    out_signs = jnp.stack([g[:2] for g in late]).astype(f32)
     summed = summed[0] + out_signs * summed[1]
     summed = (summed[:, 0] + swap_u(summed[:, 1].astype(bf), 2).astype(f32)).astype(bf)
     final = [summed[0]] + [swap_z(summed[k], k) for k in steps if k]

time: 171 us -> 148 us (0.87)
  waiting for transfers between devices: 68.8 us -> 87.5 us
  between operations: 14 us -> 0.53 us
  starting transfers between devices: 46.5 us -> 33.5 us
  local copies, waits for them, and re-layouts: 17.7 us -> 10.8 us
  Pallas kernels: 19.6 us -> 13.3 us
    ppermute x15 -> x18, waiting for transfers between devices: 48.1 us -> 72.9 us  [swap_z(): lax.ppermute(value, 'blk', [(i, i ^ 2 * step) for i in range(groups)])]
    ppermute x15 -> x18, starting transfers between devices: 35.6 us -> 24.6 us  [swap_z(): lax.ppermute(value, 'blk', [(i, i ^ 2 * step) for i in range(groups)])]
    all_gather x1 -> x0, waiting for transfers between devices: 5.37 us -> none  [stationary_plan(): lax.all_gather(sign_own, 'blk', axis=0, axis_index_groups=[[2 * i + j for...]
    unnamed x57 -> x37, local copies, waits for them, and re-layouts: 9.66 us -> 4.67 us
    pallas_call x6, Pallas kernels: 13.4 us -> 9.48 us  [the longest x2 6.98 us: project(): call(functools.partial(project_kernel, parts, size), [shape(counts[0], HE...]
    ppermute x6 -> x4, starting transfers between devices: 7.51 us -> 6.59 us  [swap_x(): return lax.ppermute(value, 'blk', [(i, i ^ 1) for i in range(groups)])]
    ppermute x6 -> x4, waiting for transfers between devices: 4.7 us -> 5.33 us  [swap_x(): return lax.ppermute(value, 'blk', [(i, i ^ 1) for i in range(groups)])]
  transfers between devices with their start and end apart: 26 -> 26, of which waited for: 16 -> 18; matrix products, arithmetic and copies ran while one was open for 5% -> 5% of each run, Pallas kernels for 8% -> 8%
where the time goes in v2:
time: 148 us
  waiting for transfers between devices  87.5 us (59%)
  starting transfers between devices  33.5 us (23%)
  Pallas kernels  13.3 us (9%)
  local copies, waits for them, and re-layouts  10.8 us (7%)
    ppermute x18, waiting for transfers between devices, swap_z(): lax.ppermute(value, 'blk', [(i, i ^ 2 * step) for i in range(groups)])  72.9 us
    ppermute x18, starting transfers between devices, swap_z(): lax.ppermute(value, 'blk', [(i, i ^ 2 * step) for i in range(groups)])  24.6 us
    ppermute x4, waiting for transfers between devices, swap_u(): return lax.ppermute(value, 'uly', [(i, i ^ bit) for i in range(team)])  9.18 us
    pallas_call x2, Pallas kernels, project(): call(functools.partial(project_kernel, parts, size), [shape(counts[0], HE...  6.98 us
    ppermute x4, starting transfers between devices, swap_x(): return lax.ppermute(value, 'blk', [(i, i ^ 1) for i in range(groups)])  6.59 us
    ppermute x4, waiting for transfers between devices, swap_x(): return lax.ppermute(value, 'blk', [(i, i ^ 1) for i in range(groups)])  5.33 us
    unnamed x37, local copies, waits for them, and re-layouts  4.67 us
    another operation x4, local copies, waits for them, and re-layouts, stationary_plan(): out_signs = jnp.stack([g[:2] for g in late]).astype(f32)  3.13 us
  transfers between devices with their start and end apart: 26, of which 18 were waited for; matrix products, arithmetic and copies ran while one was open for 5% of the time, Pallas kernels for 8%

profile of v2, /device:TPU:0, one launch (start us, length us, event | category | flops | bytes accessed | tf_op | source)
XLA Modules:
  0.0 148.1 jit_solution(16817170308201401444)
XLA Ops:
  0.0 1.7 %copy-done = bf16[2,3,320,640]{3,2,1,0:T(8,128)(2,1)S(1)} copy-done((bf16[2,3,320,640]{3,2,1,0:T(8,128)(2,1)S(1)}, bf16[2,3,320,640]{3,2,1,0:T(8,128)(2,1)}, u32[]{:S(2)}) %copy-start) | copy-done | bytes 2457624
  1.9 3.0 %collective-permute-start.5 = (bf16[2,2,320,640]{3,2,1,0:T(8,128)(2,1)S(1)}, bf16[2,2,320,640]{3,2,1,0:T(8,128)(2,1)S(1)}, u32[]{:S(2)}, u32[]{:S(2)}) collective-permute-start(bf16[2,2,320,640]{3,2,1,0:T(8,128)(2,1)S(1)} %shard_map.91), channel_id=1, source_target_pairs={{0,4},{4,0},{8,12},{12,8},{16,20},{20,16},{24,28},{28,24},{1,5},{5... | collective-permute-start | bytes 4915208 | tf_op jit(solution)/shard_map/ppermute | solution.py:354
  5.0 0.9 copy-done.6
  6.5 1.1 copy-done.3
  8.3 2.7 %collective-permute-start.6 = (bf16[3,96,640]{2,1,0:T(8,128)(2,1)S(1)}, bf16[3,96,640]{2,1,0:T(8,128)(2,1)S(1)}, u32[]{:S(2)}, u32[]{:S(2)}) collective-permute-start(bf16[3,96,640]{2,1,0:T(8,128)(2,1)S(1)} %shard_map.96.own.signs_0), channel_id=1, source_target_pairs={{0,16},{4,20},{8,24},{12,28},{16,0},{20,4},{24,8},{28,12},{1,17},{... | collective-permute-start | bytes 1105928 | tf_op jit(solution)/shard_map/ppermute | solution.py:357
  10.9 1.6 %collective-permute-start = (bf16[2,24,640]{2,1,0:T(8,128)(2,1)S(1)}, bf16[2,24,640]{2,1,0:T(8,128)(2,1)S(1)}, u32[]{:S(2)}, u32[]{:S(2)}) collective-permute-start(bf16[2,24,640]{2,1,0:T(8,128)(2,1)S(1)} %get-tuple-element.38), channel_id=1, source_target_pairs={{0,8},{4,12},{8,0},{12,4},{16,24},{20,28},{24,16},{28,20},{1,9},{5... | collective-permute-start | bytes 184328 | tf_op jit(solution)/shard_map/ppermute | solution.py:357
  12.9 2.5 %collective-permute-start.2 = (bf16[2,24,640]{2,1,0:T(8,128)(2,1)S(1)}, bf16[2,24,640]{2,1,0:T(8,128)(2,1)S(1)}, u32[]{:S(2)}, u32[]{:S(2)}) collective-permute-start(bf16[2,24,640]{2,1,0:T(8,128)(2,1)S(1)} %get-tuple-element.40), channel_id=1, source_target_pairs={{0,24},{4,28},{8,16},{12,20},{16,8},{20,12},{24,0},{28,4},{1,25},{... | collective-permute-start | bytes 184328 | tf_op jit(solution)/shard_map/ppermute | solution.py:357
  15.3 5.9 %collective-permute-done.refs_1_ = bf16[2,24,640]{2,1,0:T(8,128)(2,1)S(1)} collective-permute-done((bf16[2,24,640]{2,1,0:T(8,128)(2,1)S(1)}, bf16[2,24,640]{2,1,0:T(8,128)(2,1)S(1)}, u32[]{:S(2)}, u32[]{:S(2)}) %collective-permute-start) | collective-permute-done | bytes 61472 | tf_op jit(solution)/shard_map/ppermute | solution.py:357
  21.2 10.6 %collective-permute-done.1.refs_2_ = bf16[2,24,640]{2,1,0:T(8,128)(2,1)S(1)} collective-permute-done((bf16[2,24,640]{2,1,0:T(8,128)(2,1)S(1)}, bf16[2,24,640]{2,1,0:T(8,128)(2,1)S(1)}, u32[]{:S(2)}, u32[]{:S(2)}) %collective-permute-start.1) | collective-permute-done | bytes 61472 | tf_op jit(solution)/shard_map/ppermute | solution.py:357
  31.8 1.6 %collective-permute-start.3 = (bf16[4,2,24,640]{3,2,1,0:T(8,128)(2,1)S(1)}, bf16[4,2,24,640]{3,2,1,0:T(8,128)(2,1)S(1)}, u32[]{:S(2)}, u32[]{:S(2)}) collective-permute-start(bf16[4,2,24,640]{3,2,1,0:T(8,128)(2,1)S(1)} %shard_map.93.own), channel_id=1, source_target_pairs={{0,2},{1,3},{2,0},{3,1},{4,6},{5,7},{6,4},{7,5},{8,10},{9,11},{10,... | collective-permute-start | bytes 737288 | tf_op jit(solution)/shard_map/ppermute | solution.py:360
  33.5 1.4 collective-permute-start.7
  34.9 3.2 %collective-permute-done.3.taken = bf16[4,2,24,640]{3,2,1,0:T(8,128)(2,1)S(1)} collective-permute-done((bf16[4,2,24,640]{3,2,1,0:T(8,128)(2,1)S(1)}, bf16[4,2,24,640]{3,2,1,0:T(8,128)(2,1)S(1)}, u32[]{:S(2)}, u32[]{:S(2)}) %collective-permute-start.3) | collective-permute-done | bytes 245792 | tf_op jit(solution)/shard_map/ppermute | solution.py:360
  38.3 1.1 shard_map.99
  39.3 0.7 collective-permute-done.4.taken
  40.7 1.7 %collective-permute-start.8 = (bf16[2,320,640]{2,1,0:T(8,128)(2,1)S(1)}, bf16[2,320,640]{2,1,0:T(8,128)(2,1)S(1)}, u32[]{:S(2)}, u32[]{:S(2)}) collective-permute-start(bf16[2,320,640]{2,1,0:T(8,128)(2,1)S(1)} %get-tuple-element.46), channel_id=1, source_target_pairs={{0,4},{4,0},{8,12},{12,8},{16,20},{20,16},{24,28},{28,24},{1,5},{5... | collective-permute-start | bytes 2457608 | tf_op jit(solution)/shard_map/ppermute | solution.py:354
  42.5 8.8 %collective-permute-done.7.signs_13 = bf16[2,3,96,640]{3,2,1,0:T(8,128)(2,1)S(1)} collective-permute-done((bf16[2,3,96,640]{3,2,1,0:T(8,128)(2,1)S(1)}, bf16[2,3,96,640]{3,2,1,0:T(8,128)(2,1)S(1)}, u32[]{:S(2)}, u32[]{:S(2)}) %collective-permute-start.7) | collective-permute-done | bytes 737312 | tf_op jit(solution)/shard_map/ppermute | solution.py:357
  51.3 4.5 %shard_map.98 = (bf16[2304,128]{1,0:T(8,128)(2,1)S(1)}, f32[1536,128]{1,0:T(8,128)S(1)}, f32[768,128]{1,0:T(8,128)S(1)}) custom-call(s32[3]{0:T(128)S(1)} %pad_add_fusion.place, bf16[2,384,640]{2,1,0:T(8,128)(2,1)S(1)} %shard_map.95.rows, bf16[2,3,320,640]{3,2,1,0:T(8,128)(2,1)S(1)} %copy-done.1, ...), custom_call_target="tpu_custom_call" | custom-call | tf_op jit(solution)/shard_map/pallas_call | solution.py:407
  55.7 1.8 %collective-permute-start.10 = (bf16[2304,128]{1,0:T(8,128)(2,1)S(1)}, bf16[2304,128]{1,0:T(8,128)(2,1)S(1)}, u32[]{:S(2)}, u32[]{:S(2)}) collective-permute-start(bf16[2304,128]{1,0:T(8,128)(2,1)S(1)} %get-tuple-element.42), channel_id=1, source_target_pairs={{0,8},{4,12},{8,0},{12,4},{16,24},{20,28},{24,16},{28,20},{1,9},{5... | collective-permute-start | bytes 1769480 | tf_op jit(solution)/shard_map/ppermute | solution.py:357
  57.8 3.7 %collective-permute-start.12 = (bf16[6,24,640]{2,1,0:T(8,128)(2,1)S(1)}, bf16[6,24,640]{2,1,0:T(8,128)(2,1)S(1)}, u32[]{:S(2)}, u32[]{:S(2)}) collective-permute-start(bf16[6,24,640]{2,1,0:T(8,128)(2,1)S(1)} %get-tuple-element.55), channel_id=1, source_target_pairs={{0,16},{4,20},{8,24},{12,28},{16,0},{20,4},{24,8},{28,12},{1,17},{... | collective-permute-start | bytes 552968 | tf_op jit(solution)/shard_map/ppermute | solution.py:357
  61.9 2.5 %shard_map.100 = (bf16[960,128]{1,0:T(8,128)(2,1)S(1)}, f32[480,128]{1,0:T(8,128)S(1)}, f32[480,128]{1,0:T(8,128)S(1)}) custom-call(s32[3]{0:T(128)S(1)} %pad_add_fusion.place, bf16[2,384,640]{2,1,0:T(8,128)(2,1)S(1)} %shard_map.95.rows, bf16[2,3,320,640]{3,2,1,0:T(8,128)(2,1)S(1)} %copy-done.1, bf16[2,1,320,640]{3,2,1,0:T(8,128)(2,1)S(1)} %bitcast.73, ...), custom_call_target="tpu_custom_call" | custom-call | tf_op jit(solution)/shard_map/pallas_call | solution.py:407
  64.5 13.3 %collective-permute-done.11 = bf16[6,24,640]{2,1,0:T(8,128)(2,1)S(1)} collective-permute-done((bf16[6,24,640]{2,1,0:T(8,128)(2,1)S(1)}, bf16[6,24,640]{2,1,0:T(8,128)(2,1)S(1)}, u32[]{:S(2)}, u32[]{:S(2)}) %collective-permute-start.11) | collective-permute-done | bytes 184352 | tf_op jit(solution)/shard_map/ppermute | solution.py:357
  77.8 1.2 collective-permute-done.12
  79.0 5.9 %collective-permute-done.13 = bf16[6,24,640]{2,1,0:T(8,128)(2,1)S(1)} collective-permute-done((bf16[6,24,640]{2,1,0:T(8,128)(2,1)S(1)}, bf16[6,24,640]{2,1,0:T(8,128)(2,1)S(1)}, u32[]{:S(2)}, u32[]{:S(2)}) %collective-permute-start.13) | collective-permute-done | bytes 184352 | tf_op jit(solution)/shard_map/ppermute | solution.py:357
  86.5 0.9 slice.209
  87.5 0.9 slice.210
  88.4 0.9 slice.211
  89.3 0.9 collective-permute-start.9
  90.3 0.9 collective-permute-start.20
  91.3 11.9 %collective-permute-done.9.taken = bf16[960,128]{1,0:T(8,128)(2,1)S(1)} collective-permute-done((bf16[960,128]{1,0:T(8,128)(2,1)S(1)}, bf16[960,128]{1,0:T(8,128)(2,1)S(1)}, u32[]{:S(2)}, u32[]{:S(2)}) %collective-permute-start.9) | collective-permute-done | bytes 245792 | tf_op jit(solution)/shard_map/ppermute | solution.py:357
  103.4 0.8 shard_map.103.own
  104.1 0.9 collective-permute-start.16
  105.3 6.0 %collective-permute-done.14.taken = bf16[480,128]{1,0:T(8,128)(2,1)S(1)} collective-permute-done((bf16[480,128]{1,0:T(8,128)(2,1)S(1)}, bf16[480,128]{1,0:T(8,128)(2,1)S(1)}, u32[]{:S(2)}, u32[]{:S(2)}) %collective-permute-start.14) | collective-permute-done | bytes 122912 | tf_op jit(solution)/shard_map/ppermute | solution.py:357
  111.2 4.8 %collective-permute-done.16.partner = bf16[1536,128]{1,0:T(8,128)(2,1)S(1)} collective-permute-done((bf16[1536,128]{1,0:T(8,128)(2,1)S(1)}, bf16[1536,128]{1,0:T(8,128)(2,1)S(1)}, u32[]{:S(2)}, u32[]{:S(2)}) %collective-permute-start.16) | collective-permute-done | bytes 393248 | tf_op jit(solution)/shard_map/ppermute | solution.py:354
  116.0 1.4 shard_map.104
  117.5 1.4 collective-permute-start.17
  118.8 2.6 %collective-permute-start.18 = (bf16[480,128]{1,0:T(8,128)(2,1)S(1)}, bf16[480,128]{1,0:T(8,128)(2,1)S(1)}, u32[]{:S(2)}, u32[]{:S(2)}) collective-permute-start(bf16[480,128]{1,0:T(8,128)(2,1)S(1)} %shard_map.104), channel_id=1, source_target_pairs={{0,16},{4,20},{8,24},{12,28},{16,0},{20,4},{24,8},{28,12},{1,17},{... | collective-permute-start | bytes 368648 | tf_op jit(solution)/shard_map/ppermute | solution.py:357
  122.6 1.7 %collective-permute-done.17 = bf16[480,128]{1,0:T(8,128)(2,1)S(1)} collective-permute-done((bf16[480,128]{1,0:T(8,128)(2,1)S(1)}, bf16[480,128]{1,0:T(8,128)(2,1)S(1)}, u32[]{:S(2)}, u32[]{:S(2)}) %collective-permute-start.17) | collective-permute-done | bytes 122912 | tf_op jit(solution)/shard_map/ppermute | solution.py:357
  124.3 2.6 %collective-permute-done.18 = bf16[480,128]{1,0:T(8,128)(2,1)S(1)} collective-permute-done((bf16[480,128]{1,0:T(8,128)(2,1)S(1)}, bf16[480,128]{1,0:T(8,128)(2,1)S(1)}, u32[]{:S(2)}, u32[]{:S(2)}) %collective-permute-start.18) | collective-permute-done | bytes 122912 | tf_op jit(solution)/shard_map/ppermute | solution.py:357
  127.0 1.3 collective-permute-done.19
  130.2 0.8 slice_bitcast_fusion.7
  131.0 0.8 slice_bitcast_fusion.8
  131.8 0.8 slice_bitcast_fusion.9
  133.5 5.2 %collective-permute-done.22 = bf16[4,24,640]{2,1,0:T(8,128)(2,1)S(1)} collective-permute-done((bf16[4,24,640]{2,1,0:T(8,128)(2,1)S(1)}, bf16[4,24,640]{2,1,0:T(8,128)(2,1)S(1)}, u32[]{:S(2)}, u32[]{:S(2)}) %collective-permute-start.22) | collective-permute-done | bytes 122912 | tf_op jit(solution)/shard_map/ppermute | solution.py:360
  138.8 1.9 %collective-permute-start.23 = (bf16[24,640]{1,0:T(8,128)(2,1)S(1)}, bf16[24,640]{1,0:T(8,128)(2,1)S(1)}, u32[]{:S(2)}, u32[]{:S(2)}) collective-permute-start(bf16[24,640]{1,0:T(8,128)(2,1)S(1)} %get-tuple-element.76), channel_id=1, source_target_pairs={{0,8},{4,12},{8,0},{12,4},{16,24},{20,28},{24,16},{28,20},{1,9},{5... | collective-permute-start | bytes 92168 | tf_op jit(solution)/shard_map/ppermute | solution.py:357
  141.2 2.0 %collective-permute-start.25 = (bf16[24,640]{1,0:T(8,128)(2,1)S(1)}, bf16[24,640]{1,0:T(8,128)(2,1)S(1)}, u32[]{:S(2)}, u32[]{:S(2)}) collective-permute-start(bf16[24,640]{1,0:T(8,128)(2,1)S(1)} %get-tuple-element.74), channel_id=1, source_target_pairs={{0,24},{4,28},{8,16},{12,20},{16,8},{20,12},{24,0},{28,4},{1,25},{... | collective-permute-start | bytes 92168 | tf_op jit(solution)/shard_map/ppermute | solution.py:357
  143.2 2.5 %collective-permute-done.24.refs_2_ = bf16[24,640]{1,0:T(8,128)(2,1)S(1)} collective-permute-done((bf16[24,640]{1,0:T(8,128)(2,1)S(1)}, bf16[24,640]{1,0:T(8,128)(2,1)S(1)}, u32[]{:S(2)}, u32[]{:S(2)}) %collective-permute-start.24) | collective-permute-done | bytes 30752 | tf_op jit(solution)/shard_map/ppermute | solution.py:357
  145.7 1.1 collective-permute-done.25.refs_3_
  146.9 1.2 shard_map.105
  (92 shorter events, 9.7 us)
Async XLA Ops:
  0.0 1.7 %copy-start = (bf16[2,3,320,640]{3,2,1,0:T(8,128)(2,1)S(1)}, bf16[2,3,320,640]{3,2,1,0:T(8,128)(2,1)}, u32[]{:S(2)}) copy-start(bf16[2,3,320,640]{3,2,1,0:T(8,128)(2,1)} %weights.7) | copy-start | bytes 7372804
  1.7 3.3 %copy-start.4 = (s32[24,2560]{1,0:T(8,128)S(1)}, s32[24,2560]{1,0:T(8,128)}, u32[]{:S(2)}) copy-start(s32[24,2560]{1,0:T(8,128)} %in_bits.1) | copy-start | bytes 737284
  1.9 38.8 %collective-permute-start.5 = (bf16[2,2,320,640]{3,2,1,0:T(8,128)(2,1)S(1)}, bf16[2,2,320,640]{3,2,1,0:T(8,128)(2,1)S(1)}, u32[]{:S(2)}, u32[]{:S(2)}) collective-permute-start(bf16[2,2,320,640]{3,2,1,0:T(8,128)(2,1)S(1)} %shard_map.91), channel_id=1, source_target_pairs={{0,4},{4,0},{8,12},{12,8},{16,20},{20,16},{24,28},{28,24},{1,5},{5... | collective-permute-start | bytes 4915208 | tf_op jit(solution)/shard_map/ppermute | solution.py:354
  5.0 0.9 copy-start.6
  6.5 1.1 copy-start.3
  7.6 30.6 %copy-start.2 = (s32[96,2560]{1,0:T(8,128)S(1)}, s32[96,2560]{1,0:T(8,128)}, u32[]{:S(2)}) copy-start(s32[96,2560]{1,0:T(8,128)} %out_bits) | copy-start | bytes 2949124
  8.3 30.0 %copy-start.1 = (bf16[2,3,320,640]{3,2,1,0:T(8,128)(2,1)S(1)}, bf16[2,3,320,640]{3,2,1,0:T(8,128)(2,1)}, u32[]{:S(2)}) copy-start(bf16[2,3,320,640]{3,2,1,0:T(8,128)(2,1)} %weights.7) | copy-start | bytes 7372804
  8.3 30.0 %copy-start.5 = (s32[96,640]{1,0:T(8,128)S(1)}, s32[96,640]{1,0:T(8,128)}, u32[]{:S(2)}) copy-start(s32[96,640]{1,0:T(8,128)} %mix_bits.1) | copy-start | bytes 737284
  8.3 25.1 %collective-permute-start.6 = (bf16[3,96,640]{2,1,0:T(8,128)(2,1)S(1)}, bf16[3,96,640]{2,1,0:T(8,128)(2,1)S(1)}, u32[]{:S(2)}, u32[]{:S(2)}) collective-permute-start(bf16[3,96,640]{2,1,0:T(8,128)(2,1)S(1)} %shard_map.96.own.signs_0), channel_id=1, source_target_pairs={{0,16},{4,20},{8,24},{12,28},{16,0},{20,4},{24,8},{28,12},{1,17},{... | collective-permute-start | bytes 1105928 | tf_op jit(solution)/shard_map/ppermute | solution.py:357
  10.9 10.2 %collective-permute-start = (bf16[2,24,640]{2,1,0:T(8,128)(2,1)S(1)}, bf16[2,24,640]{2,1,0:T(8,128)(2,1)S(1)}, u32[]{:S(2)}, u32[]{:S(2)}) collective-permute-start(bf16[2,24,640]{2,1,0:T(8,128)(2,1)S(1)} %get-tuple-element.38), channel_id=1, source_target_pairs={{0,8},{4,12},{8,0},{12,4},{16,24},{20,28},{24,16},{28,20},{1,9},{5... | collective-permute-start | bytes 184328 | tf_op jit(solution)/shard_map/ppermute | solution.py:357
  12.5 19.3 %collective-permute-start.1 = (bf16[2,24,640]{2,1,0:T(8,128)(2,1)S(1)}, bf16[2,24,640]{2,1,0:T(8,128)(2,1)S(1)}, u32[]{:S(2)}, u32[]{:S(2)}) collective-permute-start(bf16[2,24,640]{2,1,0:T(8,128)(2,1)S(1)} %get-tuple-element.39), channel_id=1, source_target_pairs={{0,16},{4,20},{8,24},{12,28},{16,0},{20,4},{24,8},{28,12},{1,17},{... | collective-permute-start | bytes 184328 | tf_op jit(solution)/shard_map/ppermute | solution.py:357
  12.9 19.0 %collective-permute-start.2 = (bf16[2,24,640]{2,1,0:T(8,128)(2,1)S(1)}, bf16[2,24,640]{2,1,0:T(8,128)(2,1)S(1)}, u32[]{:S(2)}, u32[]{:S(2)}) collective-permute-start(bf16[2,24,640]{2,1,0:T(8,128)(2,1)S(1)} %get-tuple-element.40), channel_id=1, source_target_pairs={{0,24},{4,28},{8,16},{12,20},{16,8},{20,12},{24,0},{28,4},{1,25},{... | collective-permute-start | bytes 184328 | tf_op jit(solution)/shard_map/ppermute | solution.py:357
  31.8 6.3 %collective-permute-start.3 = (bf16[4,2,24,640]{3,2,1,0:T(8,128)(2,1)S(1)}, bf16[4,2,24,640]{3,2,1,0:T(8,128)(2,1)S(1)}, u32[]{:S(2)}, u32[]{:S(2)}) collective-permute-start(bf16[4,2,24,640]{3,2,1,0:T(8,128)(2,1)S(1)} %shard_map.93.own), channel_id=1, source_target_pairs={{0,2},{1,3},{2,0},{3,1},{4,6},{5,7},{6,4},{7,5},{8,10},{9,11},{10,... | collective-permute-start | bytes 737288 | tf_op jit(solution)/shard_map/ppermute | solution.py:360
  33.5 17.8 %collective-permute-start.7 = (bf16[2,3,96,640]{3,2,1,0:T(8,128)(2,1)S(1)}, bf16[2,3,96,640]{3,2,1,0:T(8,128)(2,1)S(1)}, u32[]{:S(2)}, u32[]{:S(2)}) collective-permute-start(bf16[2,3,96,640]{3,2,1,0:T(8,128)(2,1)S(1)} %shard_map.97), channel_id=1, source_target_pairs={{0,8},{4,12},{8,0},{12,4},{16,24},{20,28},{24,16},{28,20},{1,9},{5... | collective-permute-start | bytes 2211848 | tf_op jit(solution)/shard_map/ppermute | solution.py:357
  38.1 1.9 %collective-permute-start.4 = (bf16[2,4,2,24,640]{4,3,2,1,0:T(8,128)(2,1)S(1)}, bf16[2,4,2,24,640]{4,3,2,1,0:T(8,128)(2,1)S(1)}, u32[]{:S(2)}, u32[]{:S(2)}) collective-permute-start(bf16[2,4,2,24,640]{4,3,2,1,0:T(8,128)(2,1)S(1)} %shard_map.94.own), channel_id=1, source_target_pairs={{0,1},{1,0},{2,3},{3,2},{4,5},{5,4},{6,7},{7,6},{8,9},{9,8},{10,11... | collective-permute-start | bytes 1474568 | tf_op jit(solution)/shard_map/ppermute | solution.py:360
  40.7 21.2 %collective-permute-start.8 = (bf16[2,320,640]{2,1,0:T(8,128)(2,1)S(1)}, bf16[2,320,640]{2,1,0:T(8,128)(2,1)S(1)}, u32[]{:S(2)}, u32[]{:S(2)}) collective-permute-start(bf16[2,320,640]{2,1,0:T(8,128)(2,1)S(1)} %get-tuple-element.46), channel_id=1, source_target_pairs={{0,4},{4,0},{8,12},{12,8},{16,20},{20,16},{24,28},{28,24},{1,5},{5... | collective-permute-start | bytes 2457608 | tf_op jit(solution)/shard_map/ppermute | solution.py:354
  55.7 29.2 %collective-permute-start.10 = (bf16[2304,128]{1,0:T(8,128)(2,1)S(1)}, bf16[2304,128]{1,0:T(8,128)(2,1)S(1)}, u32[]{:S(2)}, u32[]{:S(2)}) collective-permute-start(bf16[2304,128]{1,0:T(8,128)(2,1)S(1)} %get-tuple-element.42), channel_id=1, source_target_pairs={{0,8},{4,12},{8,0},{12,4},{16,24},{20,28},{24,16},{28,20},{1,9},{5... | collective-permute-start | bytes 1769480 | tf_op jit(solution)/shard_map/ppermute | solution.py:357
  57.6 20.2 %collective-permute-start.11 = (bf16[6,24,640]{2,1,0:T(8,128)(2,1)S(1)}, bf16[6,24,640]{2,1,0:T(8,128)(2,1)S(1)}, u32[]{:S(2)}, u32[]{:S(2)}) collective-permute-start(bf16[6,24,640]{2,1,0:T(8,128)(2,1)S(1)} %get-tuple-element.53), channel_id=1, source_target_pairs={{0,8},{4,12},{8,0},{12,4},{16,24},{20,28},{24,16},{28,20},{1,9},{5... | collective-permute-start | bytes 552968 | tf_op jit(solution)/shard_map/ppermute | solution.py:357
  57.8 21.2 %collective-permute-start.12 = (bf16[6,24,640]{2,1,0:T(8,128)(2,1)S(1)}, bf16[6,24,640]{2,1,0:T(8,128)(2,1)S(1)}, u32[]{:S(2)}, u32[]{:S(2)}) collective-permute-start(bf16[6,24,640]{2,1,0:T(8,128)(2,1)S(1)} %get-tuple-element.55), channel_id=1, source_target_pairs={{0,16},{4,20},{8,24},{12,28},{16,0},{20,4},{24,8},{28,12},{1,17},{... | collective-permute-start | bytes 552968 | tf_op jit(solution)/shard_map/ppermute | solution.py:357
  61.5 23.5 %collective-permute-start.13 = (bf16[6,24,640]{2,1,0:T(8,128)(2,1)S(1)}, bf16[6,24,640]{2,1,0:T(8,128)(2,1)S(1)}, u32[]{:S(2)}, u32[]{:S(2)}) collective-permute-start(bf16[6,24,640]{2,1,0:T(8,128)(2,1)S(1)} %get-tuple-element.57), channel_id=1, source_target_pairs={{0,24},{4,28},{8,16},{12,20},{16,8},{20,12},{24,0},{28,4},{1,25},{... | collective-permute-start | bytes 552968 | tf_op jit(solution)/shard_map/ppermute | solution.py:357
  77.8 8.1 %copy-start.11 = (bf16[6,24,640]{2,1,0:T(8,128)(2,1)}, bf16[6,24,640]{2,1,0:T(8,128)(2,1)S(1)}, u32[]{:S(2)}) copy-start(bf16[6,24,640]{2,1,0:T(8,128)(2,1)S(1)} %collective-permute-done.11) | copy-start | bytes 552964
  79.0 5.9 %copy-start.12 = (bf16[6,24,640]{2,1,0:T(8,128)(2,1)}, bf16[6,24,640]{2,1,0:T(8,128)(2,1)S(1)}, u32[]{:S(2)}) copy-start(bf16[6,24,640]{2,1,0:T(8,128)(2,1)S(1)} %collective-permute-done.12) | copy-start | bytes 552964
  84.9 0.7 copy-start.13
  85.6 4.7 %copy-start.9 = (bf16[2,640,320]{1,2,0:T(8,128)(2,1)S(1)}, bf16[2,640,320]{1,2,0:T(8,128)(2,1)}, u32[]{:S(2)}) copy-start(bf16[2,640,320]{1,2,0:T(8,128)(2,1)} %param.15) | copy-start | bytes 2457604
  85.8 17.6 %collective-permute-start.15 = (bf16[1536,128]{1,0:T(8,128)(2,1)S(1)}, bf16[1536,128]{1,0:T(8,128)(2,1)S(1)}, u32[]{:S(2)}, u32[]{:S(2)}) collective-permute-start(bf16[1536,128]{1,0:T(8,128)(2,1)S(1)} %get-tuple-element.63), channel_id=1, source_target_pairs={{0,16},{4,20},{8,24},{12,28},{16,0},{20,4},{24,8},{28,12},{1,17},{... | collective-permute-start | bytes 1179656 | tf_op jit(solution)/shard_map/ppermute | solution.py:357
  87.4 15.9 %copy-start.7 = (f32[640]{0:T(1024)S(1)}, f32[640]{0:T(1024)}, u32[]{:S(2)}) copy-start(f32[640]{0:T(1024)} %param.14) | copy-start | bytes 7684
  89.3 14.0 %collective-permute-start.9 = (bf16[960,128]{1,0:T(8,128)(2,1)S(1)}, bf16[960,128]{1,0:T(8,128)(2,1)S(1)}, u32[]{:S(2)}, u32[]{:S(2)}) collective-permute-start(bf16[960,128]{1,0:T(8,128)(2,1)S(1)} %get-tuple-element.49), channel_id=1, source_target_pairs={{0,8},{4,12},{8,0},{12,4},{16,24},{20,28},{24,16},{28,20},{1,9},{5... | collective-permute-start | bytes 737288 | tf_op jit(solution)/shard_map/ppermute | solution.py:357
  90.3 31.7 %collective-permute-start.20 = (bf16[2,320,640]{2,1,0:T(8,128)(2,1)S(1)}, bf16[2,320,640]{2,1,0:T(8,128)(2,1)S(1)}, u32[]{:S(2)}, u32[]{:S(2)}) collective-permute-start(bf16[2,320,640]{2,1,0:T(8,128)(2,1)S(1)} %bitcast.77), channel_id=1, source_target_pairs={{0,4},{4,0},{8,12},{12,8},{16,20},{20,16},{24,28},{28,24},{1,5},{5... | collective-permute-start | bytes 2457608 | tf_op jit(solution)/shard_map/ppermute | solution.py:354
  91.3 24.7 %copy-start.8 = (f32[640]{0:T(1024)S(1)}, f32[640]{0:T(1024)}, u32[]{:S(2)}) copy-start(f32[640]{0:T(1024)} %param.13) | copy-start | bytes 7684
  104.1 11.9 %collective-permute-start.16 = (bf16[1536,128]{1,0:T(8,128)(2,1)S(1)}, bf16[1536,128]{1,0:T(8,128)(2,1)S(1)}, u32[]{:S(2)}, u32[]{:S(2)}) collective-permute-start(bf16[1536,128]{1,0:T(8,128)(2,1)S(1)} %shard_map.103.own), channel_id=1, source_target_pairs={{0,4},{4,0},{8,12},{12,8},{16,20},{20,16},{24,28},{28,24},{1,5},{5... | collective-permute-start | bytes 1179656 | tf_op jit(solution)/shard_map/ppermute | solution.py:354
  105.1 6.1 %collective-permute-start.14 = (bf16[480,128]{1,0:T(8,128)(2,1)S(1)}, bf16[480,128]{1,0:T(8,128)(2,1)S(1)}, u32[]{:S(2)}, u32[]{:S(2)}) collective-permute-start(bf16[480,128]{1,0:T(8,128)(2,1)S(1)} %get-tuple-element.62), channel_id=1, source_target_pairs={{0,16},{4,20},{8,24},{12,28},{16,0},{20,4},{24,8},{28,12},{1,17},{... | collective-permute-start | bytes 368648 | tf_op jit(solution)/shard_map/ppermute | solution.py:357
  117.5 6.8 %collective-permute-start.17 = (bf16[480,128]{1,0:T(8,128)(2,1)S(1)}, bf16[480,128]{1,0:T(8,128)(2,1)S(1)}, u32[]{:S(2)}, u32[]{:S(2)}) collective-permute-start(bf16[480,128]{1,0:T(8,128)(2,1)S(1)} %shard_map.104), channel_id=1, source_target_pairs={{0,8},{4,12},{8,0},{12,4},{16,24},{20,28},{24,16},{28,20},{1,9},{5... | collective-permute-start | bytes 368648 | tf_op jit(solution)/shard_map/ppermute | solution.py:357
  118.8 8.0 %collective-permute-start.18 = (bf16[480,128]{1,0:T(8,128)(2,1)S(1)}, bf16[480,128]{1,0:T(8,128)(2,1)S(1)}, u32[]{:S(2)}, u32[]{:S(2)}) collective-permute-start(bf16[480,128]{1,0:T(8,128)(2,1)S(1)} %shard_map.104), channel_id=1, source_target_pairs={{0,16},{4,20},{8,24},{12,28},{16,0},{20,4},{24,8},{28,12},{1,17},{... | collective-permute-start | bytes 368648 | tf_op jit(solution)/shard_map/ppermute | solution.py:357
  121.5 6.8 %collective-permute-start.19 = (bf16[480,128]{1,0:T(8,128)(2,1)S(1)}, bf16[480,128]{1,0:T(8,128)(2,1)S(1)}, u32[]{:S(2)}, u32[]{:S(2)}) collective-permute-start(bf16[480,128]{1,0:T(8,128)(2,1)S(1)} %shard_map.104), channel_id=1, source_target_pairs={{0,24},{4,28},{8,16},{12,20},{16,8},{20,12},{24,0},{28,4},{1,25},{... | collective-permute-start | bytes 368648 | tf_op jit(solution)/shard_map/ppermute | solution.py:357
  130.0 2.8 %copy-start.10 = (bf16[1,2,24,640]{3,2,0,1:T(8,128)(2,1)S(1)}, bf16[1,2,24,640]{3,2,0,1:T(8,128)(2,1)}, u32[]{:S(2)}) copy-start(bf16[1,2,24,640]{3,2,0,1:T(8,128)(2,1)} %slice_bitcast_fusion.10) | copy-start | bytes 184324
  130.1 2.6 %collective-permute-start.21 = (bf16[2,4,2,24,640]{4,3,1,2,0:T(8,128)(2,1)S(1)}, bf16[2,4,2,24,640]{4,3,1,2,0:T(8,128)(2,1)S(1)}, u32[]{:S(2)}, u32[]{:S(2)}) collective-permute-start(bf16[2,4,2,24,640]{4,3,1,2,0:T(8,128)(2,1)S(1)} %slice.180), channel_id=1, source_target_pairs={{0,1},{1,0},{2,3},{3,2},{4,5},{5,4},{6,7},{7,6},{8,9},{9,8},{10,11... | collective-permute-start | bytes 1474568 | tf_op jit(solution)/shard_map/ppermute | solution.py:360
  132.9 5.8 %collective-permute-start.22 = (bf16[4,24,640]{2,1,0:T(8,128)(2,1)S(1)}, bf16[4,24,640]{2,1,0:T(8,128)(2,1)S(1)}, u32[]{:S(2)}, u32[]{:S(2)}) collective-permute-start(bf16[4,24,640]{2,1,0:T(8,128)(2,1)S(1)} %fusion.17), channel_id=1, source_target_pairs={{0,2},{1,3},{2,0},{3,1},{4,6},{5,7},{6,4},{7,5},{8,10},{9,11},{10,... | collective-permute-start | bytes 368648 | tf_op jit(solution)/shard_map/ppermute | solution.py:360
  138.8 4.5 %collective-permute-start.23 = (bf16[24,640]{1,0:T(8,128)(2,1)S(1)}, bf16[24,640]{1,0:T(8,128)(2,1)S(1)}, u32[]{:S(2)}, u32[]{:S(2)}) collective-permute-start(bf16[24,640]{1,0:T(8,128)(2,1)S(1)} %get-tuple-element.76), channel_id=1, source_target_pairs={{0,8},{4,12},{8,0},{12,4},{16,24},{20,28},{24,16},{28,20},{1,9},{5... | collective-permute-start | bytes 92168 | tf_op jit(solution)/shard_map/ppermute | solution.py:357
  140.6 5.1 %collective-permute-start.24 = (bf16[24,640]{1,0:T(8,128)(2,1)S(1)}, bf16[24,640]{1,0:T(8,128)(2,1)S(1)}, u32[]{:S(2)}, u32[]{:S(2)}) collective-permute-start(bf16[24,640]{1,0:T(8,128)(2,1)S(1)} %get-tuple-element.75), channel_id=1, source_target_pairs={{0,16},{4,20},{8,24},{12,28},{16,0},{20,4},{24,8},{28,12},{1,17},{... | collective-permute-start | bytes 92168 | tf_op jit(solution)/shard_map/ppermute | solution.py:357
  141.2 5.7 %collective-permute-start.25 = (bf16[24,640]{1,0:T(8,128)(2,1)S(1)}, bf16[24,640]{1,0:T(8,128)(2,1)S(1)}, u32[]{:S(2)}, u32[]{:S(2)}) collective-permute-start(bf16[24,640]{1,0:T(8,128)(2,1)S(1)} %get-tuple-element.74), channel_id=1, source_target_pairs={{0,24},{4,28},{8,16},{12,20},{16,8},{20,12},{24,0},{28,4},{1,25},{... | collective-permute-start | bytes 92168 | tf_op jit(solution)/shard_map/ppermute | solution.py:357
